TPU v7x, 256 devices: a whole 4x4x8 slice. The times are simulated.
256 devices in a mesh: wide: 32 (over y, z), narrow: 8 (over x, core).
Axes of the slice: x: 4, y: 4, z: 8, core: 2. Of those that a mesh axis runs over, the one named last changes fastest.
Arguments:
- density_blocks: float32 [6144, 128, 128], P(('wide', 'narrow')), may hold values from -0.4 to 0.4
- block_groups: int32 [6144, 2], P(('wide', 'narrow')), may hold values from 0 to 63
- block_brick: int32 [6144], P(('wide', 'narrow')), may hold values from 0 to 32767, as said below
- orbital_freq: float32 [3, 8192], replicated, may hold values from 0.1 to 2
- orbital_phase: float32 [3, 8192], replicated, may hold values from -3.140625 to 3.140625
- core_density: float32 [32, 1024, 1024], P('wide', None, 'narrow'), may hold values from 0.2 to 2
Outputs:
- xc_spectrum: float32 [32, 2, 1024, 512], P('wide', None, 'narrow')
Inputs may be any that keep to these rules, and one draw needn't show every extreme that they name: `block_brick`: every block stored on the device of narrow index n has its brick within the columns n * 1024 / 8 to (n + 1) * 1024 / 8 - 1 of the grid. The blocks of one device have at most 2 bricks, counted with repeats, in the planes of any one index of wide, and some device has exactly 2.
All inputs are finite; a program needn't handle non-finite values.
Results may differ from a plain program's by a relative error of at most 0.0003.
Values sent between devices are 32-bit elements; how exact they have to be, the bound alone decides.
A program may use at most 64 MiB of HBM per device.

v0:
```python
import math

import jax
import jax.numpy as jnp
from jax import lax
from jax.sharding import PartitionSpec as P

NX = 1024
NY = 1024
GRP = 128
BY = 32
BX = 32


energy_coef = -0.75 * (3.0 / math.pi) ** (1.0 / 3.0)


def brick_pieces(blocks, group_pairs, brick_ids, orbital_freq, orbital_phase):
    row_bricks = NX // BX
    col_bricks = NY // BY
    column_block = brick_ids % row_bricks
    remainder = brick_ids // row_bricks
    row_block = remainder % col_bricks
    plane_index = remainder // col_bricks
    freq_groups = orbital_freq.reshape(3, -1, GRP)
    shift_groups = orbital_phase.reshape(3, -1, GRP)
    y_cells = (row_block * BY)[:, None] + jnp.arange(BY, dtype=jnp.int32)[None, :]
    x_cells = (column_block * BX)[:, None] + jnp.arange(BX, dtype=jnp.int32)[None, :]

    def orbital_values(group_ids):
        frequency = jnp.take(freq_groups, group_ids, axis=1)
        phase_shift = jnp.take(shift_groups, group_ids, axis=1)
        along_y = jnp.cos(
            y_cells.astype(jnp.float32)[:, :, None] * frequency[1][:, None, :]
            + phase_shift[1][:, None, :]
        )
        along_x = jnp.cos(
            x_cells.astype(jnp.float32)[:, :, None] * frequency[0][:, None, :]
            + phase_shift[0][:, None, :]
        )
        along_z = jnp.cos(plane_index.astype(jnp.float32)[:, None] * frequency[2] + phase_shift[2])
        orbital_table = along_y[:, :, None, :] * along_x[:, None, :, :] * along_z[:, None, None, :]
        return orbital_table.reshape(group_ids.shape[0], BY * BX, GRP)

    left_values = orbital_values(group_pairs[:, 0])
    right_values = orbital_values(group_pairs[:, 1])
    mixed_rows = jnp.einsum(
        "sci,sij->scj",
        left_values,
        blocks,
        precision=lax.Precision.HIGHEST,
        preferred_element_type=jnp.float32,
    )
    return jnp.sum(mixed_rows * right_values, axis=2)


def blocked_pieces(blocks, group_pairs, brick_ids, orbital_freq, orbital_phase):
    block_count = blocks.shape[0]
    step_size = math.gcd(block_count, 8)
    width = blocks.shape[1]

    def one_batch(inputs):
        return brick_pieces(inputs[0], inputs[1], inputs[2], orbital_freq, orbital_phase)

    batched = (
        blocks.reshape(block_count // step_size, step_size, width, width),
        group_pairs.reshape(block_count // step_size, step_size, 2),
        brick_ids.reshape(block_count // step_size, step_size),
    )
    return lax.map(one_batch, batched).reshape(block_count, BY * BX)


def home_place(brick_ids, plane_count, column_bricks, narrow_index):
    row_bricks = NX // BX
    col_bricks = NY // BY
    column_block = brick_ids % row_bricks
    remainder = brick_ids // row_bricks
    row_block = remainder % col_bricks
    plane_index = remainder // col_bricks
    home_index = plane_index // plane_count
    local_brick = (plane_index % plane_count * col_bricks + row_block) * column_bricks + (
        column_block - narrow_index * column_bricks
    )
    return (home_index, local_brick)


def pack_slots(home_index, wide_size, pair_slots):
    onehot = (home_index[:, None] == jnp.arange(wide_size, dtype=jnp.int32)[None, :]).astype(
        jnp.int32
    )
    slot_rank = jnp.sum((jnp.cumsum(onehot, axis=0) - 1) * onehot, axis=1)
    return home_index * pair_slots + slot_rank


def add_into_bricks(pieces, local_brick, brick_count):
    onehot = (local_brick[None, :] == jnp.arange(brick_count, dtype=jnp.int32)[:, None]).astype(
        jnp.float32
    )
    return jnp.dot(
        onehot, pieces, precision=lax.Precision.HIGHEST, preferred_element_type=jnp.float32
    )


def dft_tables(length, kept):
    points = jnp.arange(length, dtype=jnp.int32)
    waves = jnp.arange(kept, dtype=jnp.int32)
    turns = points[:, None] * waves[None, :] % length
    angle = 2.0 * math.pi / length * turns.astype(jnp.float32)
    scale = 1.0 / math.sqrt(length)
    return (jnp.cos(angle) * scale, jnp.sin(angle) * scale)


def local(density_blocks, block_groups, block_brick, orbital_freq, orbital_phase, core_density):
    wide_size = lax.axis_size("wide")
    narrow_index = lax.axis_index("narrow")
    block_count = density_blocks.shape[0]
    pair_slots = (2 * block_count + wide_size - 1) // wide_size
    slot_total = wide_size * pair_slots
    plane_count, grid_rows, column_count = core_density.shape
    column_bricks = column_count // BX
    brick_count = plane_count * (grid_rows // BY) * column_bricks
    home_index, local_brick = home_place(block_brick, plane_count, column_bricks, narrow_index)
    send_slot = pack_slots(home_index, wide_size, pair_slots)
    own_pieces = blocked_pieces(
        density_blocks, block_groups, block_brick, orbital_freq, orbital_phase
    )
    send_pieces = jnp.zeros((slot_total, BY * BX), jnp.float32).at[send_slot].set(own_pieces)
    send_local = jnp.full((slot_total,), -1, jnp.int32).at[send_slot].set(local_brick)
    pieces, got_local = (
        lax.all_to_all(send_pieces, "wide", split_axis=0, concat_axis=0, tiled=True),
        lax.all_to_all(send_local, "wide", split_axis=0, concat_axis=0, tiled=True),
    )
    brick_sums = add_into_bricks(pieces, got_local, brick_count)
    valence = (
        brick_sums.reshape(plane_count, grid_rows // BY, column_bricks, BY, BX)
        .transpose(0, 1, 3, 2, 4)
        .reshape(plane_count, grid_rows, column_count)
    )
    rho_total = core_density + valence
    energy = energy_coef * (rho_total * jnp.cbrt(rho_total) - core_density * jnp.cbrt(core_density))
    cos_x, sin_x = dft_tables(NX, NX // 2)
    cos_y, sin_y = dft_tables(NY, NY)
    x_table = jnp.stack([cos_x, -sin_x], axis=1)
    half_x = jnp.einsum(
        "zyx,xck->zcyk",
        lax.all_to_all(energy, "narrow", split_axis=1, concat_axis=2, tiled=True),
        x_table,
        precision=lax.Precision.HIGHEST,
        preferred_element_type=jnp.float32,
    )
    lines = lax.all_to_all(half_x, "narrow", split_axis=3, concat_axis=2, tiled=True)
    first_part = jnp.einsum(
        "zcyk,yq->zcqk",
        lines,
        cos_y,
        precision=lax.Precision.HIGHEST,
        preferred_element_type=jnp.float32,
    )
    second_part = jnp.einsum(
        "zcyk,yq->zcqk",
        lines,
        sin_y,
        precision=lax.Precision.HIGHEST,
        preferred_element_type=jnp.float32,
    )
    real_part = first_part[:, 0] + second_part[:, 1]
    imag_part = first_part[:, 1] - second_part[:, 0]
    columns_done = jnp.stack([real_part, imag_part], axis=1)
    return lax.all_to_all(columns_done, "narrow", split_axis=2, concat_axis=3, tiled=True)


def solution(mesh):
    return jax.shard_map(
        local,
        mesh=mesh,
        in_specs=(
            P(("wide", "narrow"), None, None),
            P(("wide", "narrow"), None),
            P(("wide", "narrow")),
            P(),
            P(),
            P("wide", None, "narrow"),
        ),
        out_specs=P("wide", None, "narrow", None),
        check_vma=False,
    )
```

profile of v0, /device:TPU:1, one launch (start us, length us, event | category | flops | bytes accessed | tf_op | source)
XLA Modules:
  0.0 222.2 jit_solution(4775553566573499595)
XLA Ops:
  2.4 12.0 %all-to-all-start = ((s32[32,2,1]{1,2,0:T(1,128)}), s32[32,2,1]{1,2,0:T(1,128)S(1)}, u32[]{:S(2)}, u32[]{:S(2)}) async-start(s32[32,2,1]{1,2,0:T(1,128)} %bitcast.26), calls=%async_computation | async-start | bytes 32768 | tf_op jit(solution)/shard_map/all_to_all | solution.py:131
  15.2 1.9 copy.52
  17.8 80.1 %while.13 = (s32[]{:T(128)}, f32[3,8,1024]{2,1,0:T(8,128)S(1)}, s32[3,8]{1,0:T(4,128)S(1)}, f32[3,8192]{1,0:T(4,128)}, s32[3,8,2]{1,0,2:T(4,128)S(1)}, /*index=5...) while((s32[]{:T(128)}, f32[3,8,1024]{2,1,0:T(8,128)S(1)}, s32[3,8]{1,0:T(4,128)S(1)}, ...), condition=%wide.region_5.7_spmd, body=%wide.region_3.6_spmd.sunk | while | flops 1617178112 | bytes 35574700 | solution.py:70
  17.8 1.5 gather_fusion
  19.4 1.5 gather_fusion.1
  20.9 1.5 gather_fusion.2
  22.4 1.5 gather_fusion.3
  24.1 0.9 add_cosine_fusion.7
  25.1 0.9 add_cosine_fusion.6
  26.7 2.3 %bitcast_multiply_fusion.2 = f32[8,1024,128]{2,1,0:T(8,128)} fusion(f32[8,32,32,128]{3,2,1,0:T(8,128)S(1)} %broadcast_multiply_fusion.5, f32[8,128]{1,0:T(8,128)S(1)} %get-tuple-element.297), kind=kLoop, calls=%fused_computation.6.clone.1 | loop fusion | flops 1048576 | bytes 8392704 | tf_op jit(solution)/shard_map/while/body/eval_jaxpr/mul | solution.py:42
  29.0 2.5 %broadcast_multiply_fusion.4 = f32[8,32,32,128]{3,2,1,0:T(8,128)} fusion(f32[8,32,128]{2,1,0:T(8,128)S(1)} %get-tuple-element.286, f32[8,32,128]{2,1,0:T(8,128)S(1)} %get-tuple-element.292), kind=kLoop, calls=%fused_computation.8.clone.1 | loop fusion | flops 1048576 | bytes 4456448 | tf_op jit(solution)/shard_map/while/body/eval_jaxpr/mul | solution.py:42
  31.5 5.4 %copy.85 = f32[8,1024,128]{1,2,0:T(8,128)} copy(f32[8,1024,128]{2,1,0:T(8,128)} %bitcast.173) | data formatting | bytes 8388608 | tf_op jit(solution)/shard_map/while/body/eval_jaxpr/mul | solution.py:42
  36.9 7.6 %multiply_reduce_fusion.2 = f32[8,1024]{1,0:T(8,128)S(1)} fusion(f32[8,1024,128]{1,2,0:T(8,128)} %copy.85, f32[8,1024,128]{2,1,0:T(8,128)} %bitcast_multiply_fusion.2, f32[8,128]{1,0:T(8,128)S(1)} %get-tuple-element.298, f32[3,8,128,128]{2,3,1,0:T(8,128)S(1)} %get-tuple-element.321, s32[]{:T(128)} %get-tuple-element.307), kind=kOutput, calls=%fused_computation.7.clone.1 | convolution fusion | flops 1613750272 | bytes 8949764 | tf_op jit(solution)/shard_map/while/body/eval_jaxpr/sci,sij->scj/dot_general | solution.py:47
  44.6 1.5 gather_fusion
  46.1 1.5 gather_fusion.1
  47.5 1.5 gather_fusion.2
  49.1 1.5 gather_fusion.3
  51.8 0.9 add_cosine_fusion.6
  53.4 2.3 %bitcast_multiply_fusion.2 = f32[8,1024,128]{2,1,0:T(8,128)} fusion(f32[8,32,32,128]{3,2,1,0:T(8,128)S(1)} %broadcast_multiply_fusion.5, f32[8,128]{1,0:T(8,128)S(1)} %get-tuple-element.297), kind=kLoop, calls=%fused_computation.6.clone.1 | loop fusion | flops 1048576 | bytes 8392704 | tf_op jit(solution)/shard_map/while/body/eval_jaxpr/mul | solution.py:42
  55.7 2.5 %broadcast_multiply_fusion.4 = f32[8,32,32,128]{3,2,1,0:T(8,128)} fusion(f32[8,32,128]{2,1,0:T(8,128)S(1)} %get-tuple-element.286, f32[8,32,128]{2,1,0:T(8,128)S(1)} %get-tuple-element.292), kind=kLoop, calls=%fused_computation.8.clone.1 | loop fusion | flops 1048576 | bytes 4456448 | tf_op jit(solution)/shard_map/while/body/eval_jaxpr/mul | solution.py:42
  58.2 5.4 %copy.85 = f32[8,1024,128]{1,2,0:T(8,128)} copy(f32[8,1024,128]{2,1,0:T(8,128)} %bitcast.173) | data formatting | bytes 8388608 | tf_op jit(solution)/shard_map/while/body/eval_jaxpr/mul | solution.py:42
  63.6 7.6 %multiply_reduce_fusion.2 = f32[8,1024]{1,0:T(8,128)S(1)} fusion(f32[8,1024,128]{1,2,0:T(8,128)} %copy.85, f32[8,1024,128]{2,1,0:T(8,128)} %bitcast_multiply_fusion.2, f32[8,128]{1,0:T(8,128)S(1)} %get-tuple-element.298, f32[3,8,128,128]{2,3,1,0:T(8,128)S(1)} %get-tuple-element.321, s32[]{:T(128)} %get-tuple-element.307), kind=kOutput, calls=%fused_computation.7.clone.1 | convolution fusion | flops 1613750272 | bytes 8949764 | tf_op jit(solution)/shard_map/while/body/eval_jaxpr/sci,sij->scj/dot_general | solution.py:47
  71.3 1.5 gather_fusion
  72.7 1.5 gather_fusion.1
  74.2 1.5 gather_fusion.2
  75.8 1.5 gather_fusion.3
  78.5 0.9 add_cosine_fusion.6
  80.1 2.3 %bitcast_multiply_fusion.2 = f32[8,1024,128]{2,1,0:T(8,128)} fusion(f32[8,32,32,128]{3,2,1,0:T(8,128)S(1)} %broadcast_multiply_fusion.5, f32[8,128]{1,0:T(8,128)S(1)} %get-tuple-element.297), kind=kLoop, calls=%fused_computation.6.clone.1 | loop fusion | flops 1048576 | bytes 8392704 | tf_op jit(solution)/shard_map/while/body/eval_jaxpr/mul | solution.py:42
  82.4 2.5 %broadcast_multiply_fusion.4 = f32[8,32,32,128]{3,2,1,0:T(8,128)} fusion(f32[8,32,128]{2,1,0:T(8,128)S(1)} %get-tuple-element.286, f32[8,32,128]{2,1,0:T(8,128)S(1)} %get-tuple-element.292), kind=kLoop, calls=%fused_computation.8.clone.1 | loop fusion | flops 1048576 | bytes 4456448 | tf_op jit(solution)/shard_map/while/body/eval_jaxpr/mul | solution.py:42
  84.9 5.4 %copy.85 = f32[8,1024,128]{1,2,0:T(8,128)} copy(f32[8,1024,128]{2,1,0:T(8,128)} %bitcast.173) | data formatting | bytes 8388608 | tf_op jit(solution)/shard_map/while/body/eval_jaxpr/mul | solution.py:42
  90.3 7.6 %multiply_reduce_fusion.2 = f32[8,1024]{1,0:T(8,128)S(1)} fusion(f32[8,1024,128]{1,2,0:T(8,128)} %copy.85, f32[8,1024,128]{2,1,0:T(8,128)} %bitcast_multiply_fusion.2, f32[8,128]{1,0:T(8,128)S(1)} %get-tuple-element.298, f32[3,8,128,128]{2,3,1,0:T(8,128)S(1)} %get-tuple-element.321, s32[]{:T(128)} %get-tuple-element.307), kind=kOutput, calls=%fused_computation.7.clone.1 | convolution fusion | flops 1613750272 | bytes 8949764 | tf_op jit(solution)/shard_map/while/body/eval_jaxpr/sci,sij->scj/dot_general | solution.py:47
  99.5 9.4 %all-to-all-start.1 = ((f32[32,2,1024]{2,1,0:T(2,128)}), f32[32,2,1024]{2,1,0:T(2,128)S(1)}, u32[]{:S(2)}, u32[]{:S(2)}) async-start(f32[32,2,1024]{2,1,0:T(2,128)} %all_to_all.51), calls=%async_computation.1 | async-start | bytes 524288 | tf_op jit(solution)/shard_map/all_to_all | solution.py:130
  110.4 7.9 %all-to-all-done.1 = f32[32,2,1024]{2,1,0:T(2,128)S(1)} async-done(((f32[32,2,1024]{2,1,0:T(2,128)}), f32[32,2,1024]{2,1,0:T(2,128)S(1)}, u32[]{:S(2)}, u32[]{:S(2)}) %all-to-all-start.1) | async-done | bytes 262176 | tf_op jit(solution)/shard_map/all_to_all | solution.py:130
  118.8 2.7 %convolution_bitcast_fusion = f32[1,32,32,4,32]{4,1,2,3,0:T(8,128)} fusion(f32[32,32,64,1]{2,1,0,3:T(8,128)S(1)} %bitcast.177, s32[32,4]{0,1:T(4,128)S(1)} %multiply_add_fusion, s32[64]{0:T(128)S(1)} %eq.55), kind=kOutput, calls=%fused_computation.95 | convolution fusion | flops 100671488 | bytes 787200 | tf_op jit(solution)/shard_map/dot_general | solution.py:99
  121.5 3.2 %copy.55 = f32[1,32,32,4,32]{2,1,4,3,0:T(8,128)S(1)} copy(f32[1,32,32,4,32]{4,1,2,3,0:T(8,128)} %convolution_bitcast_fusion) | data formatting | bytes 1048576 | tf_op jit(solution)/shard_map/transpose | solution.py:136
  124.7 1.0 reshape.409
  126.5 1.0 copy.59
  127.6 7.9 %all-to-all-start.2 = ((f32[1,1024,128]{2,0,1:T(1,128)}), f32[1,1024,128]{2,0,1:T(1,128)S(1)}, u32[]{:S(2)}, u32[]{:S(2)}) async-start(f32[1,1024,128]{2,0,1:T(1,128)} %copy.59), calls=%async_computation.2 | async-start | bytes 1048576 | tf_op jit(solution)/shard_map/all_to_all | solution.py:146
  135.5 9.1 %multiply_negate_fusion = (f32[1024,1,512]{0,2,1:T(8,128)S(1)}, f32[1024,1,512]{0,2,1:T(8,128)}) fusion(), kind=kLoop, calls=%fused_computation.88 | loop fusion | flops 8912896 | bytes 4194304 | tf_op jit(solution)/shard_map/neg | solution.py:143
  145.4 5.0 %fusion.41 = f32[1,2,128,512]{2,3,1,0:T(8,128)S(1)} fusion(f32[128,1024,1]{1,0,2:T(8,128)S(1)} %reshape.476, f32[1024,1,512]{0,2,1:T(8,128)S(1)} %get-tuple-element.200, f32[1024,1,512]{0,2,1:T(8,128)} %get-tuple-element.201), kind=kOutput, calls=%fused_computation.96 | convolution fusion | flops 1611661312 | bytes 5242880 | tf_op jit(solution)/shard_map/zyx,xck->zcyk/dot_general | solution.py:144
  150.8 13.6 %all_to_all.69 = f32[1,2,128,512]{2,1,0,3:T(2,128)S(1)} all-to-all(f32[1,2,128,512]{2,1,0,3:T(2,128)S(1)} %copy.61), channel_id=1, replica_groups=mesh['wide'=32,'narrow'=8] {'narrow'}, dimensions={3} | all-to-all | bytes 1048576 | tf_op jit(solution)/shard_map/all_to_all | solution.py:151
  164.8 18.6 %fusion.25 = f32[1024,128]{0,1:S(1)} fusion(f32[1024,128]{0,1:T(8,128)S(1)} %bitcast.187), kind=kOutput, calls=%fused_computation.76 | convolution fusion | flops 1626341376 | bytes 1048576
  183.4 18.7 %fusion.22 = f32[1024,128]{0,1:S(1)} fusion(f32[1024,128]{0,1:T(8,128)S(1)} %bitcast.188), kind=kOutput, calls=%fused_computation.73 | convolution fusion | flops 1626341376 | bytes 1048576
  202.8 1.1 reshape.495
  203.9 12.8 %all_to_all.70 = f32[8,1,16384]{2,1,0:T(1,128)S(1)} all-to-all(f32[8,1,16384]{2,1,0:T(1,128)S(1)} %reshape.495), channel_id=1, replica_groups=mesh['wide'=32,'narrow'=8] {'narrow'}, dimensions={0} | all-to-all | bytes 1048576 | tf_op jit(solution)/shard_map/all_to_all | solution.py:169
  217.2 1.9 reduce.4
  219.9 1.2 copy.64
  221.2 1.0 copy.66
  (89 shorter events, 16.8 us)
Async XLA Ops:
  2.4 97.1 %all-to-all-start = ((s32[32,2,1]{1,2,0:T(1,128)}), s32[32,2,1]{1,2,0:T(1,128)S(1)}, u32[]{:S(2)}, u32[]{:S(2)}) async-start(s32[32,2,1]{1,2,0:T(1,128)} %bitcast.26), calls=%async_computation | async-start | bytes 32768 | tf_op jit(solution)/shard_map/all_to_all | solution.py:131
  17.8 91.1 %copy-start = (f32[1,1024,128]{2,1,0:T(8,128)S(1)}, f32[1,1024,128]{2,1,0:T(8,128)}, u32[]{:S(2)}) copy-start(f32[1,1024,128]{2,1,0:T(8,128)} %param.15) | copy-start | bytes 1572868
  99.5 18.9 %all-to-all-start.1 = ((f32[32,2,1024]{2,1,0:T(2,128)}), f32[32,2,1024]{2,1,0:T(2,128)S(1)}, u32[]{:S(2)}, u32[]{:S(2)}) async-start(f32[32,2,1024]{2,1,0:T(2,128)} %all_to_all.51), calls=%async_computation.1 | async-start | bytes 524288 | tf_op jit(solution)/shard_map/all_to_all | solution.py:130
  127.6 17.4 %all-to-all-start.2 = ((f32[1,1024,128]{2,0,1:T(1,128)}), f32[1,1024,128]{2,0,1:T(1,128)S(1)}, u32[]{:S(2)}, u32[]{:S(2)}) async-start(f32[1,1024,128]{2,0,1:T(1,128)} %copy.59), calls=%async_computation.2 | async-start | bytes 1048576 | tf_op jit(solution)/shard_map/all_to_all | solution.py:146
where the time goes:
time: 223 us; the launch traced here: 222 us
  matrix products  67.7 us (30%)
  local copies, waits for them, and re-layouts  53.2 us (24%)
  other arithmetic  36.6 us (16%)
  starting transfers between devices  29.4 us (13%)
  blocking collectives  26.4 us (12%)
  waiting for transfers between devices  8.28 us (4%)
    unnamed x2, matrix products  37.2 us
    dot_general x3, matrix products, brick_pieces(): jnp.einsum('sci,sij->scj', left_values, blocks, precision=lax.Precision.H...  22.7 us
    mul x3, local copies, waits for them, and re-layouts, orbital_values(): along_y[:, :, None, :] * along_x[:, None, :, :] * along_z[:, None, None, :]  16.1 us
    mul x9, other arithmetic, orbital_values(): along_y[:, :, None, :] * along_x[:, None, :, :] * along_z[:, None, None, :]  16 us
    all_to_all x1, blocking collectives, local(): lax.all_to_all(half_x, 'narrow', split_axis=3, concat_axis=2, tiled=True)  13.6 us
    all_to_all x1, blocking collectives, local(): lax.all_to_all(columns_done, 'narrow', split_axis=2, concat_axis=3, tiled...  12.8 us
    all_to_all x1, starting transfers between devices, local(): lax.all_to_all(send_local, 'wide', split_axis=0, concat_axis=0, tiled=True)  12 us
    all_to_all x1, starting transfers between devices, local(): lax.all_to_all(send_pieces, 'wide', split_axis=0, concat_axis=0, tiled=True)  9.4 us
  transfers between devices with their start and end apart: 3, of which 2 were waited for; matrix products, arithmetic and copies ran while one was open for 43% of the time, Pallas kernels for 0%

commit v1 on v0

v1 whole, which is shorter than its diff:
```python
import functools
import math

import jax
import jax.numpy as jnp
import ml_dtypes
import numpy as np
from jax import lax
from jax.experimental import pallas as pl
from jax.experimental.pallas import tpu as pltpu
from jax.sharding import PartitionSpec as P

NX = 1024
NY = 1024
GRP = 128
BY = 32
BX = 32
MESH = pl.DeviceIdType.MESH

energy_coef = -0.75 * (3.0 / math.pi) ** (1.0 / 3.0)

INV_TURN = 1.0 / (2.0 * math.pi)
PI_HI = 3.140625
PI_LO = math.pi - PI_HI
SINE = (
    2.604579135698264e-06,
    -0.00019808792785020506,
    0.008333047269825162,
    -0.16666657833027024,
    0.9999999956345141,
)


def cosine(angle):
    turns = jnp.round(angle * INV_TURN)
    half = (0.5 * angle - turns * PI_HI) - turns * PI_LO
    square = half * half
    poly = SINE[0]
    for coef in SINE[1:]:
        poly = poly * square + coef
    sine = half * poly
    return 1.0 - 2.0 * (sine * sine)


def split(value):
    high = value.astype(jnp.bfloat16)
    return high, (value - high.astype(jnp.float32)).astype(jnp.bfloat16)


def power43(value):
    return jnp.exp(jnp.log(value) * (4.0 / 3.0))


def split_table(table):
    table = np.asarray(table, np.float32)
    high = table.astype(ml_dtypes.bfloat16)
    low = (table - high.astype(np.float32)).astype(ml_dtypes.bfloat16)
    return np.stack([high, low])


def y_tables(parts):
    rows = NY // parts
    col = np.arange(NY // 2)
    y = (col % 16) * 32 + (col // 16 % 4) * 8 + col // 64
    ky = (
        np.arange(parts)[:, None, None] * rows
        + np.arange(2)[None, :, None]
        + 2 * np.arange(rows // 2)[None, None, :]
    )
    angle = 2.0 * np.pi / NY * (ky[..., None] * y % NY)
    return split_table(
        np.concatenate([np.cos(angle), -np.sin(angle)], 2) / math.sqrt(NY)
    )


def x_tables(chips):
    x = np.arange(NX).reshape(chips, NX // chips)
    kx = np.arange(NX // 2)
    angle = 2.0 * np.pi / NX * (x[..., None] * kx % NX)
    return split_table(
        np.concatenate([np.cos(angle), np.sin(angle)], 1) / math.sqrt(NX)
    )


def one_piece(b, groups_ref, brick_ref, waves_ref, block):
    brick = brick_ref[b]
    x0 = ((brick & 31) * BX).astype(jnp.float32)
    y0 = (((brick >> 5) & 31) * BY).astype(jnp.float32)
    z0 = (brick >> 10).astype(jnp.float32)
    step = lax.broadcasted_iota(jnp.int32, (32, GRP), 0).astype(jnp.float32)
    xs, ys = step + x0, step + y0

    def tables(side):
        wave = waves_ref[groups_ref[b, side]]
        along_x = cosine(xs * wave[0:1] + wave[3:4])
        along_y = cosine(ys * wave[1:2] + wave[4:5])
        along_z = cosine(z0 * wave[2:3] + wave[5:6])
        return along_x * along_z, along_y

    left_x, left_y = tables(0)
    right_x, right_y = tables(1)
    high, low = split(block)
    weights = jnp.concatenate(
        [
            jnp.concatenate([high, low], 1),
            jnp.concatenate([high, jnp.zeros_like(low)], 1),
        ],
        0,
    )
    lane = lax.broadcasted_iota(jnp.int32, (32, 8, 128), 2)
    at_x = lax.broadcasted_iota(jnp.int32, (32, 8, 128), 0)
    total = jnp.zeros((8, 128), jnp.float32)
    for part in range(4):
        rows = slice(part * 8, part * 8 + 8)
        left = (left_x[:, None, :] * left_y[None, rows, :]).reshape(256, GRP)
        right = right_x[:, None, :] * right_y[None, rows, :]
        mixed = jnp.dot(
            jnp.concatenate(split(left), 1), weights, preferred_element_type=jnp.float32
        )
        mixed = (mixed[:, :GRP] + mixed[:, GRP:]).reshape(32, 8, GRP) * right
        sums = jnp.sum(mixed, axis=2, keepdims=True)
        total = total + jnp.sum(
            jnp.where(lane == at_x + part * 32, sums, 0.0), axis=0
        )
    return total


def whole_kernel(
    n_wide,
    n_narrow,
    n_blocks,
    groups_ref,
    brick_ref,
    freq_ref,
    phase_ref,
    blocks_hbm,
    core_hbm,
    ytab_hbm,
    xtab_hbm,
    out_ref,
    blocks_ref,
    core_ref,
    ytab_ref,
    xtab_ref,
    waves_ref,
    brick_col,
    piece_ref,
    place_send,
    place_recv,
    send_ref,
    recv_ref,
    core_pow,
    fold_ref,
    half_send,
    half_recv,
    acc_ref,
    load_sem,
    place_ssem,
    place_rsem,
    piece_ssem,
    piece_rsem,
    half_ssem,
    half_rsem,
):
    wide, narrow = lax.axis_index("wide"), lax.axis_index("narrow")
    loads = [
        pltpu.make_async_copy(src, dst, load_sem.at[i])
        for i, (src, dst) in enumerate(
            (
                (blocks_hbm, blocks_ref),
                (core_hbm, core_ref),
                (ytab_hbm, ytab_ref),
                (xtab_hbm, xtab_ref),
            )
        )
    ]
    for load in loads:
        load.start()

    barrier = pltpu.get_barrier_semaphore()

    def greet_wide(d, carry):
        peer = lax.rem(wide + d, n_wide)
        pl.semaphore_signal(
            barrier, inc=1, device_id=(peer, narrow), device_id_type=MESH
        )
        return carry

    def greet_narrow(d, carry):
        peer = lax.rem(narrow + d, n_narrow)
        pl.semaphore_signal(
            barrier, inc=1, device_id=(wide, peer), device_id_type=MESH
        )
        return carry

    lax.fori_loop(1, n_wide, greet_wide, 0)
    lax.fori_loop(1, n_narrow, greet_narrow, 0)

    brick_col[...] = jnp.zeros_like(brick_col)

    def spread(b, carry):
        brick_col[pl.ds(b, 1), :] = jnp.full((1, 128), brick_ref[b], jnp.int32)
        return carry

    lax.fori_loop(0, n_blocks, spread, 0)
    bricks = brick_col[...]
    row = lax.broadcasted_iota(jnp.int32, (128, 128), 0)
    lane = lax.broadcasted_iota(jnp.int32, (128, 128), 1)
    home = jnp.where(row < n_blocks, bricks // 1024, -1)
    home_t = jnp.transpose(home.astype(jnp.float32)).astype(jnp.int32)
    rank = jnp.sum(
        jnp.where((home == home_t) & (lane < row), 1.0, 0.0), axis=1, keepdims=True
    ).astype(jnp.int32)
    slot = jnp.where(row < n_blocks, 2 * home + rank, -1)
    slot_t = jnp.transpose(slot.astype(jnp.float32)).astype(jnp.int32)
    place = (bricks % 4 * 32 + bricks // 32 % 32 + 1).astype(jnp.bfloat16)
    wide_row = lax.broadcasted_iota(jnp.int32, (n_wide * 8, 128), 0)
    wanted = jnp.where(wide_row % 8 < 2, wide_row // 8 * 2 + wide_row % 8, -2)
    pick8 = jnp.where(
        jnp.broadcast_to(slot_t[0:1], (n_wide * 8, 128)) == wanted, 1.0, 0.0
    ).astype(jnp.bfloat16)
    place_send[...] = (
        jnp.dot(pick8, place, preferred_element_type=jnp.float32) - 1.0
    )
    slot_row = lax.broadcasted_iota(jnp.int32, (2 * n_wide, 128), 0)
    pick = jnp.where(
        jnp.broadcast_to(slot_t[0:1], (2 * n_wide, 128)) == slot_row, 1.0, 0.0
    ).astype(jnp.bfloat16)[:, :32]
    pick = jnp.concatenate([pick, pick], 1)

    pl.semaphore_wait(barrier, n_wide + n_narrow - 2)

    def place_copy(d):
        peer = lax.rem(wide + d, n_wide)
        return pltpu.make_async_remote_copy(
            src_ref=place_send.at[pl.ds(pl.multiple_of(peer * 8, 8), 8)],
            dst_ref=place_recv.at[pl.ds(pl.multiple_of(wide * 8, 8), 8)],
            send_sem=place_ssem.at[d],
            recv_sem=place_rsem.at[d],
            device_id=(peer, narrow),
            device_id_type=MESH,
        )

    def start_place(d, carry):
        place_copy(d).start()
        return carry

    lax.fori_loop(1, n_wide, start_place, 0)
    own8 = pl.ds(pl.multiple_of(wide * 8, 8), 8)
    place_recv[own8] = place_send[own8]

    for g in range(waves_ref.shape[0]):
        at = slice(g * GRP, g * GRP + GRP)
        waves_ref[g, 0:3, :] = freq_ref[:, at]
        waves_ref[g, 3:6, :] = phase_ref[:, at]
        waves_ref[g, 6:8, :] = jnp.zeros((2, GRP), jnp.float32)
    loads[0].wait()
    piece_ref[...] = jnp.zeros_like(piece_ref)

    def work(b, carry):
        piece_ref[pl.ds(pl.multiple_of(b * 8, 8), 8), :] = one_piece(
            b, groups_ref, brick_ref, waves_ref, blocks_ref[b]
        )
        return carry

    lax.fori_loop(0, n_blocks, work, 0)
    for r in range(8):
        high, low = split(piece_ref[pl.ds(r, 32, stride=8), :])
        send_ref[pl.ds(r, 2 * n_wide, stride=8), :] = jnp.dot(
            pick, jnp.concatenate([high, low], 0), preferred_element_type=jnp.float32
        )

    def piece_copy(d):
        peer = lax.rem(wide + d, n_wide)
        return pltpu.make_async_remote_copy(
            src_ref=send_ref.at[pl.ds(pl.multiple_of(peer * 16, 16), 16)],
            dst_ref=recv_ref.at[pl.ds(pl.multiple_of(wide * 16, 16), 16)],
            send_sem=piece_ssem.at[d],
            recv_sem=piece_rsem.at[d],
            device_id=(peer, narrow),
            device_id_type=MESH,
        )

    def start_piece(d, carry):
        piece_copy(d).start()
        return carry

    lax.fori_loop(1, n_wide, start_piece, 0)
    own16 = pl.ds(pl.multiple_of(wide * 16, 16), 16)
    recv_ref[own16] = send_ref[own16]

    loads[1].wait()
    for r in range(8):
        for part in range(4):
            core_pow[pl.ds((r * 4 + part) * 32, 32), :] = power43(
                core_ref[pl.ds(part * 8 + r, 32, stride=32), :]
            )

    def wait_place(d, carry):
        place_copy(d).wait()
        return carry

    lax.fori_loop(1, n_wide, wait_place, 0)
    brick_lane = lax.broadcasted_iota(jnp.int32, (n_wide, 128), 1).astype(jnp.float32)
    spots = [
        jnp.where(place_recv[pl.ds(k, n_wide, stride=8), :] == brick_lane, 1.0, 0.0)
        for k in range(2)
    ]
    gather = jnp.transpose(jnp.concatenate([*spots, *spots], 0)).astype(jnp.bfloat16)

    def wait_piece(d, carry):
        piece_copy(d).wait()
        return carry

    lax.fori_loop(1, n_wide, wait_piece, 0)
    group = lax.broadcasted_iota(jnp.int32, (32, 128), 1) // 32
    for r in range(8):
        got = jnp.concatenate(
            [recv_ref[pl.ds(k * 8 + r, n_wide, stride=16), :] for k in range(2)], 0
        )
        high, low = split(got)
        sums = jnp.dot(
            gather, jnp.concatenate([high, low], 0), preferred_element_type=jnp.float32
        )
        for part in range(4):
            valence = None
            for c in range(4):
                turned = sums[c * 32 : c * 32 + 32]
                if c != part:
                    turned = pltpu.roll(turned, (c - part) % 4 * 32, 1)
                valence = turned if c == 0 else jnp.where(group == c, turned, valence)
            rho = core_ref[pl.ds(part * 8 + r, 32, stride=32), :] + valence
            energy = energy_coef * (
                power43(jnp.abs(rho)) - core_pow[pl.ds((r * 4 + part) * 32, 32), :]
            )
            for parity in range(2):
                fold = (
                    energy[:16] + energy[16:]
                    if parity == 0
                    else energy[:16] - energy[16:]
                )
                fold_ref[parity, pl.ds((r * 4 + part) * 16, 16), :] = jnp.concatenate(
                    split(fold), 1
                )

    loads[2].wait()
    chips = n_narrow // 2

    def half_copy(i, peer):
        return pltpu.make_async_remote_copy(
            src_ref=half_send.at[peer],
            dst_ref=half_recv.at[narrow],
            send_sem=half_ssem.at[i],
            recv_sem=half_rsem.at[i],
            device_id=(wide, peer),
            device_id_type=MESH,
        )

    hops = [(2, 0), (2, 1), (1, 0), (3, 0), (1, 1), (3, 1), (0, 1), (0, 0)]

    def peer_at(hop):
        chip = lax.rem(narrow // 2 + hop[0], chips)
        return chip * 2 + lax.rem(narrow + hop[1], 2)

    for i, hop in enumerate(hops):
        peer = peer_at(hop)
        target = half_send.at[peer] if hop != (0, 0) else half_recv.at[narrow]
        for parity in range(2):
            spread_y = jnp.dot(
                ytab_ref[0, peer, parity],
                fold_ref[parity],
                preferred_element_type=jnp.float32,
            )
            half = (
                spread_y[:, :128]
                + spread_y[:, 128:]
                + jnp.dot(
                    ytab_ref[1, peer, parity],
                    fold_ref[parity, :, 0:128],
                    preferred_element_type=jnp.float32,
                )
            )
            target[pl.ds(parity, 64, stride=2), :] = half[:64]
            target[pl.ds(128 + parity, 64, stride=2), :] = half[64:]
        if hop != (0, 0):
            half_copy(i, peer).start()

    loads[3].wait()
    waits = {0: (6,), 1: (3, 5), 3: (2, 4), 2: (0, 1)}
    for n, (on, copies) in enumerate(waits.items()):
        for i in copies:
            half_copy(i, peer_at(hops[i])).wait_recv()
        chip = lax.rem(narrow // 2 + on, chips)
        columns = jnp.concatenate([half_recv[2 * chip], half_recv[2 * chip + 1]], 1)
        real, imag = columns[:128], columns[128:]
        high, low = split(
            jnp.concatenate(
                [
                    jnp.concatenate([real, imag], 1),
                    jnp.concatenate([imag, -real], 1),
                ],
                0,
            )
        )
        part = (
            jnp.dot(high, xtab_ref[0, chip], preferred_element_type=jnp.float32)
            + jnp.dot(low, xtab_ref[0, chip], preferred_element_type=jnp.float32)
            + jnp.dot(high, xtab_ref[1, chip], preferred_element_type=jnp.float32)
        )
        if n == 0:
            acc_ref[...] = part
        elif n < 3:
            acc_ref[...] += part
        else:
            total = acc_ref[...] + part
            for c in range(2):
                out_ref[0, c] = total[c * 128 : c * 128 + 128]

    for i in range(len(hops) - 1):
        half_copy(i, peer_at(hops[i])).wait_send()


def local(density_blocks, block_groups, block_brick, orbital_freq, orbital_phase, core_density):
    n_wide, n_narrow = lax.axis_size("wide"), lax.axis_size("narrow")
    n_blocks = density_blocks.shape[0]
    ytab, xtab = y_tables(n_narrow), x_tables(n_narrow // 2)
    vmem = pl.BlockSpec(memory_space=pltpu.VMEM)
    smem = pl.BlockSpec(memory_space=pltpu.SMEM)
    hbm = pl.BlockSpec(memory_space=pl.ANY)
    f32, bf16 = jnp.float32, jnp.bfloat16
    rows = NY // n_narrow
    return pl.pallas_call(
        functools.partial(whole_kernel, n_wide, n_narrow, n_blocks),
        out_shape=jax.ShapeDtypeStruct((1, 2, rows, NX // 2), f32),
        in_specs=[smem, smem, vmem, vmem, hbm, hbm, hbm, hbm],
        out_specs=vmem,
        scratch_shapes=[
            pltpu.VMEM(density_blocks.shape, f32),
            pltpu.VMEM(core_density.shape[1:], f32),
            pltpu.VMEM(ytab.shape, bf16),
            pltpu.VMEM(xtab.shape, bf16),
            pltpu.VMEM((orbital_freq.shape[1] // GRP, 8, GRP), f32),
            pltpu.VMEM((128, 128), jnp.int32),
            pltpu.VMEM((32 * 8, 128), f32),
            pltpu.VMEM((n_wide * 8, 128), f32),
            pltpu.VMEM((n_wide * 8, 128), f32),
            pltpu.VMEM((n_wide * 16, 128), f32),
            pltpu.VMEM((n_wide * 16, 128), f32),
            pltpu.VMEM((NY, 128), f32),
            pltpu.VMEM((2, NY // 2, 256), bf16),
            pltpu.VMEM((n_narrow, 256, 128), f32),
            pltpu.VMEM((n_narrow, 256, 128), f32),
            pltpu.VMEM((256, NX // 2), f32),
            pltpu.SemaphoreType.DMA((4,)),
            pltpu.SemaphoreType.DMA((n_wide,)),
            pltpu.SemaphoreType.DMA((n_wide,)),
            pltpu.SemaphoreType.DMA((n_wide,)),
            pltpu.SemaphoreType.DMA((n_wide,)),
            pltpu.SemaphoreType.DMA((n_narrow,)),
            pltpu.SemaphoreType.DMA((n_narrow,)),
        ],
        compiler_params=pltpu.CompilerParams(
            collective_id=0, has_side_effects=True, vmem_limit_bytes=48 * 2**20
        ),
    )(
        block_groups,
        block_brick,
        orbital_freq,
        orbital_phase,
        density_blocks,
        core_density.reshape(core_density.shape[1:]),
        jnp.asarray(ytab),
        jnp.asarray(xtab),
    )


def solution(mesh):
    return jax.shard_map(
        local,
        mesh=mesh,
        in_specs=(
            P(("wide", "narrow"), None, None),
            P(("wide", "narrow"), None),
            P(("wide", "narrow")),
            P(),
            P(),
            P("wide", None, "narrow"),
        ),
        out_specs=P("wide", None, "narrow", None),
        check_vma=False,
    )
```

time: 223 us -> 54 us (0.24)
  matrix products: 67.7 us -> 0 us
  Pallas kernels: 0 us -> 47.3 us
  local copies, waits for them, and re-layouts: 53.2 us -> 6.46 us
  other arithmetic: 36.6 us -> 0 us
  starting transfers between devices: 29.4 us -> 0 us
  blocking collectives: 26.4 us -> 0 us
  waiting for transfers between devices: 8.28 us -> 0 us
    pallas_call x0 -> x1, Pallas kernels: none -> 47.3 us  [local(): pl.pallas_call(functools.partial(whole_kernel, n_wide, n_narrow, n_blocks...]
    unnamed x2 -> x0, matrix products: 37.2 us -> none
    dot_general x5 -> x0, matrix products: 30.5 us -> none  [the longest x3 22.7 us: brick_pieces(): jnp.einsum('sci,sij->scj', left_values, blocks, precision=lax.Precision.H...]
    all_to_all x3 -> x0, starting transfers between devices: 29.4 us -> none  [the longest x1 12 us: local(): lax.all_to_all(send_local, 'wide', split_axis=0, concat_axis=0, tiled=True)]
    all_to_all x2 -> x0, blocking collectives: 26.4 us -> none  [the longest x1 13.6 us: local(): lax.all_to_all(half_x, 'narrow', split_axis=3, concat_axis=2, tiled=True)]
    gather x12 -> x0, local copies, waits for them, and re-layouts: 17.8 us -> none  [the longest x6 8.93 us: orbital_values(): frequency = jnp.take(freq_groups, group_ids, axis=1)]
    mul x7 -> x0, local copies, waits for them, and re-layouts: 17.1 us -> none  [the longest x3 16.1 us: orbital_values(): along_y[:, :, None, :] * along_x[:, None, :, :] * along_z[:, None, None, :]]
    mul x13 -> x0, other arithmetic: 17 us -> none  [the longest x9 16 us: orbital_values(): along_y[:, :, None, :] * along_x[:, None, :, :] * along_z[:, None, None, :]]
  transfers between devices with their start and end apart: 3 -> 0, of which waited for: 2 -> 0; matrix products, arithmetic and copies ran while one was open for 43% -> 0% of each run, Pallas kernels for 0% -> 0%
where the time goes in v1:
time: 54 us; the launch traced here: 53.8 us
  Pallas kernels  47.3 us (88%)
  local copies, waits for them, and re-layouts  6.46 us (12%)
    pallas_call x1, Pallas kernels, local(): pl.pallas_call(functools.partial(whole_kernel, n_wide, n_narrow, n_blocks...  47.3 us
    unnamed x12, local copies, waits for them, and re-layouts  6.46 us

profile of v1, /device:TPU:1, one launch (start us, length us, event | category | flops | bytes accessed | tf_op | source)
XLA Modules:
  0.0 53.8 jit_solution(1344488577045100082)
XLA Ops:
  0.0 0.8 %copy.9.groups_ref = s32[24,2]{1,0:T(8,128)S(1)} copy(s32[24,2]{0,1:T(2,128)} %param.9) | data formatting | bytes 384 | tf_op args[1]
  0.8 0.0 copy-start
  0.8 1.4 %copy-done = f32[24,128,128]{2,1,0:T(8,128)S(1)} copy-done((f32[24,128,128]{2,1,0:T(8,128)S(1)}, f32[24,128,128]{2,1,0:T(8,128)}, u32[]{:S(2)}) %copy-start) | copy-done | bytes 1572888
  2.2 0.0 copy-start.1
  2.2 1.0 %copy-done.1 = f32[1,1024,128]{2,1,0:T(8,128)S(1)} copy-done((f32[1,1024,128]{2,1,0:T(8,128)S(1)}, f32[1,1024,128]{2,1,0:T(8,128)}, u32[]{:S(2)}) %copy-start.1) | copy-done | bytes 524312
  3.2 0.0 copy-start.2
  3.2 0.9 %copy-done.2 = f32[3,8192]{1,0:T(4,128)S(1)} copy-done((f32[3,8192]{1,0:T(4,128)S(1)}, f32[3,8192]{1,0:T(4,128)}, u32[]{:S(2)}) %copy-start.2) | copy-done | bytes 98328
  4.1 0.0 copy-start.3
  4.1 0.9 %copy-done.3 = f32[3,8192]{1,0:T(4,128)S(1)} copy-done((f32[3,8192]{1,0:T(4,128)S(1)}, f32[3,8192]{1,0:T(4,128)}, u32[]{:S(2)}) %copy-start.3) | copy-done | bytes 98328
  5.0 0.0 copy-start.4
  5.0 0.7 %copy-done.4 = s32[24]{0:T(128)S(1)} copy-done((s32[24]{0:T(128)S(1)}, s32[24]{0:T(128)}, u32[]{:S(2)}) %copy-start.4) | copy-done | bytes 120
  5.7 47.3 %shard_map.82 = f32[1,2,128,512]{3,2,1,0:T(8,128)S(1)} custom-call(s32[24,2]{1,0:T(8,128)S(1)} %copy.9.groups_ref, s32[24]{0:T(128)S(1)} %copy-done.4, f32[3,8192]{1,0:T(4,128)S(1)} %copy-done.2, f32[3,8192]{1,0:T(4,128)S(1)} %copy-done.3, f32[24,128,128]{2,1,0:T(8,128)S(1)} %copy-done, f32[1024,128]{1,0:T(8,128)S(1)} %bitcast.1, ...), custom_call_target="tpu_custom_call" | custom-call | tf_op jit(solution)/shard_map/pallas_call | solution.py:432
  53.0 0.8 %copy.11 = f32[1,2,128,512]{3,2,1,0:T(8,128)} copy(f32[1,2,128,512]{3,2,1,0:T(8,128)S(1)} %shard_map.82) | data formatting | bytes 1048576
Async XLA Ops:
  0.8 1.4 %copy-start = (f32[24,128,128]{2,1,0:T(8,128)S(1)}, f32[24,128,128]{2,1,0:T(8,128)}, u32[]{:S(2)}) copy-start(f32[24,128,128]{2,1,0:T(8,128)} %blocks_hbm.1) | copy-start | bytes 4718596
  2.2 1.0 %copy-start.1 = (f32[1,1024,128]{2,1,0:T(8,128)S(1)}, f32[1,1024,128]{2,1,0:T(8,128)}, u32[]{:S(2)}) copy-start(f32[1,1024,128]{2,1,0:T(8,128)} %param.13) | copy-start | bytes 1572868
  3.2 0.9 %copy-start.2 = (f32[3,8192]{1,0:T(4,128)S(1)}, f32[3,8192]{1,0:T(4,128)}, u32[]{:S(2)}) copy-start(f32[3,8192]{1,0:T(4,128)} %freq_ref.1) | copy-start | bytes 294916
  4.1 0.9 %copy-start.3 = (f32[3,8192]{1,0:T(4,128)S(1)}, f32[3,8192]{1,0:T(4,128)}, u32[]{:S(2)}) copy-start(f32[3,8192]{1,0:T(4,128)} %phase_ref.1) | copy-start | bytes 294916
  5.0 0.7 %copy-start.4 = (s32[24]{0:T(128)S(1)}, s32[24]{0:T(128)}, u32[]{:S(2)}) copy-start(s32[24]{0:T(128)} %brick_ref.1) | copy-start | bytes 292

commit v2 on v1

v2 whole, which is shorter than its diff:
```python
import functools
import math

import jax
import jax.numpy as jnp
import ml_dtypes
import numpy as np
from jax import lax
from jax.experimental import pallas as pl
from jax.experimental.pallas import tpu as pltpu
from jax.sharding import PartitionSpec as P

NX = 1024
NY = 1024
GRP = 128
BY = 32
BX = 32
MESH = pl.DeviceIdType.MESH

energy_coef = -0.75 * (3.0 / math.pi) ** (1.0 / 3.0)

INV_TURN = 1.0 / (2.0 * math.pi)
PI_HI = 3.140625
PI_LO = math.pi - PI_HI
SINE = (
    2.604579135698264e-06,
    -0.00019808792785020506,
    0.008333047269825162,
    -0.16666657833027024,
    0.9999999956345141,
)


def cosine(angle):
    turns = jnp.round(angle * INV_TURN)
    half = (0.5 * angle - turns * PI_HI) - turns * PI_LO
    square = half * half
    poly = SINE[0]
    for coef in SINE[1:]:
        poly = poly * square + coef
    sine = half * poly
    return 1.0 - 2.0 * (sine * sine)


def split(value):
    high = value.astype(jnp.bfloat16)
    return high, (value - high.astype(jnp.float32)).astype(jnp.bfloat16)


def power43(value):
    return jnp.exp(jnp.log(value) * (4.0 / 3.0))


def split_table(table):
    table = np.asarray(table, np.float32)
    high = table.astype(ml_dtypes.bfloat16)
    low = (table - high.astype(np.float32)).astype(ml_dtypes.bfloat16)
    return np.stack([high, low])


def y_tables(parts):
    rows = NY // parts
    col = np.arange(NY // 2)
    r, g = col // 128, col // 16 % 8
    y = col % 16 * 32 + g % 4 * 8 + 2 * r + g // 4
    ky = (
        np.arange(parts)[:, None, None] * rows
        + np.arange(2)[None, :, None]
        + 2 * np.arange(rows // 2)[None, None, :]
    )
    angle = 2.0 * np.pi / NY * (ky[..., None] * y % NY)
    return split_table(
        np.concatenate([np.cos(angle), -np.sin(angle)], 2) / math.sqrt(NY)
    )


def x_tables(chips):
    h, chip, core, xb, xi = np.ix_(*map(np.arange, (2, chips, 2, 4, 16)))
    x = (chip * 2 + core) * 128 + xb * 32 + h * 16 + xi
    x = x.reshape(2, chips, 2, 64, 1)
    angle = 2.0 * np.pi / NX * (x * np.arange(NX // 2) % NX)
    both = np.stack([np.cos(angle), np.sin(angle)], 3) / math.sqrt(NX)
    return split_table(both.reshape(2, chips, 256, NX // 2))


def block_tables(b, groups_ref, brick_ref, waves_ref, blocks_ref, factor_ref, weight_ref):
    brick = brick_ref[b]
    x0 = ((brick & 31) * BX).astype(jnp.float32)
    y0 = (((brick >> 5) & 31) * BY).astype(jnp.float32)
    z0 = (brick >> 10).astype(jnp.float32)
    step = lax.broadcasted_iota(jnp.int32, (32, GRP), 0).astype(jnp.float32)
    xs, ys = step + x0, step + y0
    for side in range(2):
        wave = waves_ref[groups_ref[side, b]]
        along_z = cosine(z0 * wave[2:3] + wave[5:6])
        factor_ref[b, 2 * side] = cosine(xs * wave[0:1] + wave[3:4]) * along_z
        factor_ref[b, 2 * side + 1] = cosine(ys * wave[1:2] + wave[4:5])
    high, low = split(blocks_ref[b])
    weight_ref[b] = jnp.concatenate(
        [
            jnp.concatenate([high, low], 1),
            jnp.concatenate([high, jnp.zeros_like(low)], 1),
        ],
        0,
    )


def half_piece(b, h, factor_ref, weight_ref):
    cols = slice(h * 16, h * 16 + 16)
    left_x, right_x = factor_ref[b, 0, cols], factor_ref[b, 2, cols]
    weights = weight_ref[b]
    shape = (2, 16, 8, GRP)
    lane = lax.broadcasted_iota(jnp.int32, shape, 3) & 63
    spot = lax.broadcasted_iota(jnp.int32, shape, 1) + 16 * lax.broadcasted_iota(
        jnp.int32, shape, 0
    )
    total = jnp.zeros((8, 128), jnp.float32)
    for part in range(2):
        rows = slice(part * 16, part * 16 + 16)
        left_y = factor_ref[b, 1, rows].reshape(2, 1, 8, GRP)
        right_y = factor_ref[b, 3, rows].reshape(2, 1, 8, GRP)
        left = (left_x[None, :, None, :] * left_y).reshape(256, GRP)
        right = right_x[None, :, None, :] * right_y
        mixed = jnp.dot(
            jnp.concatenate(split(left), 1), weights, preferred_element_type=jnp.float32
        )
        mixed = (mixed[:, :GRP] + mixed[:, GRP:]).reshape(shape) * right
        sums = jnp.sum(mixed, axis=3, keepdims=True)
        total = total + jnp.sum(
            jnp.where(lane == spot + part * 32, sums, 0.0), axis=(0, 1)
        )
    return total


def whole_kernel(
    n_wide,
    n_narrow,
    n_blocks,
    groups_ref,
    brick_ref,
    freq_hbm,
    phase_hbm,
    blocks_hbm,
    core_hbm,
    ytab_hbm,
    xtab_hbm,
    out_ref,
    freq_ref,
    phase_ref,
    blocks_ref,
    core_ref,
    ytab_ref,
    xtab_ref,
    waves_ref,
    factor_ref,
    weight_ref,
    brick_col,
    piece_ref,
    place_send,
    place_recv,
    send_ref,
    recv_ref,
    core_part,
    core_pow,
    fold_ref,
    half_send,
    half_recv,
    acc_ref,
    load_sem,
    place_ssem,
    place_rsem,
    piece_ssem,
    piece_rsem,
    half_ssem,
    half_rsem,
):
    wide, narrow = lax.axis_index("wide"), lax.axis_index("narrow")
    loads = [
        pltpu.make_async_copy(src, dst, load_sem.at[i])
        for i, (src, dst) in enumerate(
            (
                (freq_hbm, freq_ref),
                (phase_hbm, phase_ref),
                (blocks_hbm, blocks_ref),
                (core_hbm, core_ref),
                (ytab_hbm, ytab_ref),
                (xtab_hbm, xtab_ref),
            )
        )
    ]
    for load in loads:
        load.start()

    barrier = pltpu.get_barrier_semaphore()

    def greet_wide(d, carry):
        peer = lax.rem(wide + d, n_wide)
        pl.semaphore_signal(
            barrier, inc=1, device_id=(peer, narrow), device_id_type=MESH
        )
        return carry

    def greet_narrow(d, carry):
        peer = lax.rem(narrow + d, n_narrow)
        pl.semaphore_signal(
            barrier, inc=1, device_id=(wide, peer), device_id_type=MESH
        )
        return carry

    lax.fori_loop(1, n_wide, greet_wide, 0)
    lax.fori_loop(1, n_narrow, greet_narrow, 0)

    brick_col[...] = jnp.zeros_like(brick_col)

    def spread(b, carry):
        brick_col[pl.ds(b, 1), :] = jnp.full((1, 128), brick_ref[b], jnp.int32)
        return carry

    lax.fori_loop(0, n_blocks, spread, 0)
    bricks = brick_col[...]
    row = lax.broadcasted_iota(jnp.int32, (128, 128), 0)
    lane = lax.broadcasted_iota(jnp.int32, (128, 128), 1)
    home = jnp.where(row < n_blocks, bricks >> 10, -1)
    home_t = jnp.transpose(home.astype(jnp.float32)).astype(jnp.int32)
    rank = jnp.sum(
        jnp.where((home == home_t) & (lane < row), 1.0, 0.0), axis=1, keepdims=True
    ).astype(jnp.int32)
    slot = jnp.where(row < n_blocks, 2 * home + rank, -1)
    slot_t = jnp.transpose(slot.astype(jnp.float32)).astype(jnp.int32)
    by = (bricks >> 5) & 31
    place = ((by >> 4) * 64 + (bricks & 3) * 16 + (by & 15) + 1).astype(jnp.bfloat16)
    wide_row = lax.broadcasted_iota(jnp.int32, (n_wide * 8, 128), 0)
    wanted = jnp.where((wide_row & 7) < 2, (wide_row >> 3) * 2 + (wide_row & 7), -2)
    pick8 = jnp.where(
        jnp.broadcast_to(slot_t[0:1], (n_wide * 8, 128)) == wanted, 1.0, 0.0
    ).astype(jnp.bfloat16)
    place_send[...] = (
        jnp.dot(pick8, place, preferred_element_type=jnp.float32) - 1.0
    )
    slot_row = lax.broadcasted_iota(jnp.int32, (2 * n_wide, 128), 0)
    slot_row = jnp.where(slot_row < n_wide, 2 * slot_row, 2 * (slot_row - n_wide) + 1)
    pick = jnp.where(
        jnp.broadcast_to(slot_t[0:1], (2 * n_wide, 128)) == slot_row, 1.0, 0.0
    ).astype(jnp.bfloat16)[:, :32]
    pick = jnp.concatenate([pick, pick], 1)

    loads[0].wait()
    loads[1].wait()
    for g in range(waves_ref.shape[0]):
        at = slice(g * GRP, g * GRP + GRP)
        waves_ref[g, 0:3, :] = freq_ref[:, at]
        waves_ref[g, 3:6, :] = phase_ref[:, at]
        waves_ref[g, 6:8, :] = jnp.zeros((2, GRP), jnp.float32)
    loads[2].wait()
    piece_ref[...] = jnp.zeros_like(piece_ref)

    def prepare(b, carry):
        block_tables(
            b, groups_ref, brick_ref, waves_ref, blocks_ref, factor_ref, weight_ref
        )
        return carry

    lax.fori_loop(0, n_blocks, prepare, 0, unroll=4)

    first = lax.broadcasted_iota(jnp.int32, (32, 128), 1) < 64

    def place_copy(d):
        peer = lax.rem(wide + d, n_wide)
        return pltpu.make_async_remote_copy(
            src_ref=place_send.at[pl.ds(pl.multiple_of(peer * 8, 8), 8)],
            dst_ref=place_recv.at[pl.ds(pl.multiple_of(wide * 8, 8), 8)],
            send_sem=place_ssem.at[d],
            recv_sem=place_rsem.at[d],
            device_id=(peer, narrow),
            device_id_type=MESH,
        )

    def piece_copy(h, d):
        peer = lax.rem(wide + d, n_wide)
        return pltpu.make_async_remote_copy(
            src_ref=send_ref.at[h, pl.ds(pl.multiple_of(peer * 8, 8), 8)],
            dst_ref=recv_ref.at[h, pl.ds(pl.multiple_of(wide * 8, 8), 8)],
            send_sem=piece_ssem.at[h, d],
            recv_sem=piece_rsem.at[h, d],
            device_id=(peer, narrow),
            device_id_type=MESH,
        )

    own8 = pl.ds(pl.multiple_of(wide * 8, 8), 8)
    for h in range(2):

        def work(b, carry, h=h):
            piece_ref[h, pl.ds(pl.multiple_of(b * 8, 8), 8), :] = half_piece(
                b, h, factor_ref, weight_ref
            )
            return carry

        lax.fori_loop(0, n_blocks, work, 0, unroll=8)
        for r in range(8):
            both = jnp.concatenate(split(piece_ref[h, pl.ds(r, 32, stride=8), :]), 0)
            slots = jnp.dot(pick, both, preferred_element_type=jnp.float32)
            send_ref[h, pl.ds(r, n_wide, stride=8), :] = jnp.where(
                first, slots[:n_wide], slots[n_wide:]
            )
        if h == 0:
            pl.semaphore_wait(barrier, n_wide + n_narrow - 2)

        def start_piece(d, carry, h=h):
            piece_copy(h, d).start()
            return carry

        lax.fori_loop(1, n_wide, start_piece, 0)
        recv_ref[h, own8] = send_ref[h, own8]
        if h == 0:

            def start_place(d, carry):
                place_copy(d).start()
                return carry

            lax.fori_loop(1, n_wide, start_place, 0)
            place_recv[own8] = place_send[own8]

    loads[3].wait()
    at = lax.broadcasted_iota(jnp.int32, (256, 256), 0)
    to = (
        ((at >> 4) & 1) * 128 + (at >> 7) * 64 + ((at >> 5) & 3) * 16 + (at & 15)
    )
    order = jnp.where(
        to == lax.broadcasted_iota(jnp.int32, (256, 256), 1), 1.0, 0.0
    ).astype(jnp.bfloat16)
    for r in range(4):
        rows = []
        for g in range(8):
            y = g % 4 * 8 + 2 * r + g // 4
            rows.append(
                jnp.concatenate(
                    [core_ref[pl.ds(y + t * 512, 16, stride=32), :] for t in range(2)],
                    1,
                )
            )
        value = jnp.concatenate(rows, 0)
        high, rest = value.astype(jnp.bfloat16), value
        rest = rest - high.astype(jnp.float32)
        moved = (
            jnp.dot(high, order, preferred_element_type=jnp.float32)
            + sum(
                jnp.dot(part, order, preferred_element_type=jnp.float32)
                for part in split(rest)
            )
        )
        for h in range(2):
            own = moved[:, h * 128 : h * 128 + 128]
            core_part[h, r * 128 : r * 128 + 128, :] = own
            core_pow[h, r * 128 : r * 128 + 128, :] = power43(own)

    def wait_place(d, carry):
        place_copy(d).wait()
        return carry

    lax.fori_loop(1, n_wide, wait_place, 0)
    brick_lane = lax.broadcasted_iota(jnp.int32, (n_wide, 128), 1).astype(jnp.float32)
    spots = [
        jnp.where(place_recv[pl.ds(k, n_wide, stride=8), :] == brick_lane, 1.0, 0.0)
        for k in range(2)
    ]
    gather = jnp.transpose(jnp.concatenate([*spots, *spots], 0)).astype(jnp.bfloat16)

    chips = n_narrow // 2
    hops = [(2, 0), (2, 1), (1, 0), (3, 0), (1, 1), (3, 1), (0, 1), (0, 0)]

    def peer_at(hop):
        chip = lax.rem(narrow // 2 + hop[0], chips)
        return chip * 2 + lax.rem(narrow + hop[1], 2)

    def half_copy(h, i):
        peer = peer_at(hops[i])
        return pltpu.make_async_remote_copy(
            src_ref=half_send.at[h, peer],
            dst_ref=half_recv.at[h, narrow],
            send_sem=half_ssem.at[h, i],
            recv_sem=half_rsem.at[h, i],
            device_id=(wide, peer),
            device_id_type=MESH,
        )

    group = lax.broadcasted_iota(jnp.int32, (16, 128), 1) >> 4
    low16 = group < 4
    low64 = lax.broadcasted_iota(jnp.int32, (64, 128), 1) < 64
    for h in range(2):

        def wait_piece(d, carry, h=h):
            piece_copy(h, d).wait()
            return carry

        lax.fori_loop(1, n_wide, wait_piece, 0)
        for r in range(4):
            even = recv_ref[h, pl.ds(2 * r, n_wide, stride=8), :]
            odd = recv_ref[h, pl.ds(2 * r + 1, n_wide, stride=8), :]
            got = jnp.concatenate(
                [
                    jnp.where(first, even, pltpu.roll(odd, 64, 1)),
                    jnp.where(first, pltpu.roll(even, 64, 1), odd),
                ],
                0,
            )
            sums = jnp.dot(
                gather,
                jnp.concatenate(split(got), 0),
                preferred_element_type=jnp.float32,
            )
            tiles = [sums[j * 16 : j * 16 + 16] for j in range(8)]
            for bit in (1, 2, 4):
                for j in range(8):
                    if not j & bit:
                        a, b = tiles[j], tiles[j | bit]
                        keep = (group & bit) == 0
                        tiles[j] = jnp.where(keep, a, pltpu.roll(b, 16 * bit, 1))
                        tiles[j | bit] = jnp.where(
                            keep, pltpu.roll(a, 128 - 16 * bit, 1), b
                        )
            for g in range(8):
                at = slice((r * 8 + g) * 16, (r * 8 + g) * 16 + 16)
                rho = core_part[h, at, :] + tiles[g]
                energy = energy_coef * (power43(jnp.abs(rho)) - core_pow[h, at, :])
                other = pltpu.roll(energy, 64, 1)
                fold = jnp.where(low16, energy + other, other - energy)
                high = fold.astype(jnp.bfloat16).astype(jnp.float32)
                rest = fold - high
                fold_ref[h, 0, at, :] = jnp.where(
                    low16, high, pltpu.roll(rest, 64, 1)
                ).astype(jnp.bfloat16)
                fold_ref[h, 1, at, :] = jnp.where(
                    low16, pltpu.roll(high, 64, 1), rest
                ).astype(jnp.bfloat16)
        if h == 0:
            loads[4].wait()
        for i, hop in enumerate(hops):
            peer = peer_at(hop)
            target = half_recv.at[h, narrow] if hop == (0, 0) else half_send.at[h, peer]
            for parity in range(2):
                half = jnp.dot(
                    ytab_ref[0, peer, parity],
                    fold_ref[h, parity],
                    preferred_element_type=jnp.float32,
                ) + jnp.dot(
                    ytab_ref[1, peer, parity],
                    fold_ref[h, parity],
                    preferred_element_type=jnp.float32,
                )
                half = half + pltpu.roll(half, 64, 1)
                target[pl.ds(parity, 64, stride=2), :] = jnp.where(
                    low64, half[:64], half[64:]
                )
            if hop != (0, 0):
                half_copy(h, i).start()

    loads[5].wait()
    low256 = (lax.broadcasted_iota(jnp.int32, (128, 256), 1) & 127) < 64
    waits = {0: (6,), 1: (3, 5), 3: (2, 4), 2: (0, 1)}
    for h in range(2):
        for on, copies in waits.items():
            for i in copies:
                half_copy(h, i).wait_recv()
            chip = lax.rem(narrow // 2 + on, chips)
            ours = [half_recv[h, 2 * chip + core] for core in range(2)]
            turned = [pltpu.roll(own, 64, 1) for own in ours]
            real, imag = jnp.concatenate(ours, 1), jnp.concatenate(turned, 1)
            high, low = split(
                jnp.concatenate([real, jnp.where(low256, imag, -imag)], 0)
            )
            part = (
                jnp.dot(high, xtab_ref[0, h, chip], preferred_element_type=jnp.float32)
                + jnp.dot(low, xtab_ref[0, h, chip], preferred_element_type=jnp.float32)
                + jnp.dot(high, xtab_ref[1, h, chip], preferred_element_type=jnp.float32)
            )
            if (h, on) == (0, 0):
                acc_ref[...] = part
            elif (h, on) != (1, 2):
                acc_ref[...] += part
            else:
                total = acc_ref[...] + part
                for c in range(2):
                    out_ref[0, c] = total[c * 128 : c * 128 + 128]

    for h in range(2):
        for i in range(len(hops) - 1):
            half_copy(h, i).wait_send()


def local(density_blocks, block_groups, block_brick, orbital_freq, orbital_phase, core_density):
    n_wide, n_narrow = lax.axis_size("wide"), lax.axis_size("narrow")
    n_blocks = density_blocks.shape[0]
    ytab, xtab = y_tables(n_narrow), x_tables(n_narrow // 2)
    vmem = pl.BlockSpec(memory_space=pltpu.VMEM)
    smem = pl.BlockSpec(memory_space=pltpu.SMEM)
    hbm = pl.BlockSpec(memory_space=pl.ANY)
    f32, bf16 = jnp.float32, jnp.bfloat16
    rows = NY // n_narrow
    return pl.pallas_call(
        functools.partial(whole_kernel, n_wide, n_narrow, n_blocks),
        out_shape=jax.ShapeDtypeStruct((1, 2, rows, NX // 2), f32),
        in_specs=[smem, smem, hbm, hbm, hbm, hbm, hbm, hbm],
        out_specs=vmem,
        scratch_shapes=[
            pltpu.VMEM(orbital_freq.shape, f32),
            pltpu.VMEM(orbital_phase.shape, f32),
            pltpu.VMEM(density_blocks.shape, f32),
            pltpu.VMEM(core_density.shape[1:], f32),
            pltpu.VMEM(ytab.shape, bf16),
            pltpu.VMEM(xtab.shape, bf16),
            pltpu.VMEM((orbital_freq.shape[1] // GRP, 8, GRP), f32),
            pltpu.VMEM((n_blocks, 4, 32, GRP), f32),
            pltpu.VMEM((n_blocks, 2 * GRP, 2 * GRP), bf16),
            pltpu.VMEM((128, 128), jnp.int32),
            pltpu.VMEM((2, 32 * 8, 128), f32),
            pltpu.VMEM((n_wide * 8, 128), f32),
            pltpu.VMEM((n_wide * 8, 128), f32),
            pltpu.VMEM((2, n_wide * 8, 128), f32),
            pltpu.VMEM((2, n_wide * 8, 128), f32),
            pltpu.VMEM((2, NY // 2, 128), f32),
            pltpu.VMEM((2, NY // 2, 128), f32),
            pltpu.VMEM((2, 2, NY // 2, 128), bf16),
            pltpu.VMEM((2, n_narrow, 128, 128), f32),
            pltpu.VMEM((2, n_narrow, 128, 128), f32),
            pltpu.VMEM((256, NX // 2), f32),
            pltpu.SemaphoreType.DMA((6,)),
            pltpu.SemaphoreType.DMA((n_wide,)),
            pltpu.SemaphoreType.DMA((n_wide,)),
            pltpu.SemaphoreType.DMA((2, n_wide)),
            pltpu.SemaphoreType.DMA((2, n_wide)),
            pltpu.SemaphoreType.DMA((2, n_narrow)),
            pltpu.SemaphoreType.DMA((2, n_narrow)),
        ],
        compiler_params=pltpu.CompilerParams(
            collective_id=0, has_side_effects=True, vmem_limit_bytes=62 * 2**20
        ),
    )(
        block_groups.T,
        block_brick,
        orbital_freq,
        orbital_phase,
        density_blocks,
        core_density.reshape(core_density.shape[1:]),
        jnp.asarray(ytab),
        jnp.asarray(xtab),
    )


def solution(mesh):
    return jax.shard_map(
        local,
        mesh=mesh,
        in_specs=(
            P(("wide", "narrow"), None, None),
            P(("wide", "narrow"), None),
            P(("wide", "narrow")),
            P(),
            P(),
            P("wide", None, "narrow"),
        ),
        out_specs=P("wide", None, "narrow", None),
        check_vma=False,
    )
```

time: 54 us -> 43.1 us (0.80)
  Pallas kernels: 47.3 us -> 41.1 us
  local copies, waits for them, and re-layouts: 6.46 us -> 1.87 us
    pallas_call x1, Pallas kernels: 47.3 us -> 41.1 us  [local(): pl.pallas_call(functools.partial(whole_kernel, n_wide, n_narrow, n_blocks...]
    unnamed x12 -> x1, local copies, waits for them, and re-layouts: 6.46 us -> 1.87 us
where the time goes in v2:
time: 43.1 us; the launch traced here: 43 us
  Pallas kernels  41.1 us (95%)
  local copies, waits for them, and re-layouts  1.87 us (4%)
    pallas_call x1, Pallas kernels, local(): pl.pallas_call(functools.partial(whole_kernel, n_wide, n_narrow, n_blocks...  41.1 us
    unnamed x1, local copies, waits for them, and re-layouts  1.87 us

profile of v2, /device:TPU:1, one launch (start us, length us, event | category | flops | bytes accessed | tf_op | source)
XLA Modules:
  0.0 43.0 jit_solution(10017956944477800494)
XLA Ops:
  0.0 41.1 %shard_map.82 = f32[1,2,128,512]{3,2,1,0:T(8,128)} custom-call(s32[2,24]{1,0:T(2,128)} %bitcast.3, s32[24]{0:T(128)} %brick_ref.1, f32[3,8192]{1,0:T(4,128)} %freq_hbm.1, f32[3,8192]{1,0:T(4,128)} %phase_hbm.1, f32[24,128,128]{2,1,0:T(8,128)} %blocks_hbm.1, f32[1024,128]{1,0:T(8,128)} %bitcast.2, bf16[2,8,2,128,512]{4,3,2,1,0:T(8,128)(2,1)} %constant.4.clone.ytab_hbm, ...), custom_call_target="tpu_custom_call" | custom-call | tf_op jit(solution)/shard_map/pallas_call | solution.py:499
  41.1 1.9 %copy.10 = f32[1,2,128,512]{3,2,1,0:T(8,128)} copy(f32[1,2,128,512]{3,2,1,0:T(8,128)} %shard_map.82) | data formatting | bytes 1048576

commit v3 on v2

--- a/solution.py
+++ b/solution.py
@@ -81,6 +81,10 @@
     angle = 2.0 * np.pi / NX * (x * np.arange(NX // 2) % NX)
     both = np.stack([np.cos(angle), np.sin(angle)], 3) / math.sqrt(NX)
     return split_table(both.reshape(2, chips, 256, NX // 2))
+
+
+def wait_all(ref, sem):
+    pltpu.make_async_copy(ref, ref, sem).wait()
 
 
 def block_tables(b, groups_ref, brick_ref, waves_ref, blocks_ref, factor_ref, weight_ref):
@@ -136,8 +140,8 @@
     n_wide,
     n_narrow,
     n_blocks,
-    groups_ref,
-    brick_ref,
+    groups_hbm,
+    brick_hbm,
     freq_hbm,
     phase_hbm,
     blocks_hbm,
@@ -145,6 +149,8 @@
     ytab_hbm,
     xtab_hbm,
     out_ref,
+    groups_ref,
+    brick_ref,
     freq_ref,
     phase_ref,
     blocks_ref,
@@ -179,6 +185,8 @@
         pltpu.make_async_copy(src, dst, load_sem.at[i])
         for i, (src, dst) in enumerate(
             (
+                (brick_hbm, brick_ref),
+                (groups_hbm, groups_ref),
                 (freq_hbm, freq_ref),
                 (phase_hbm, phase_ref),
                 (blocks_hbm, blocks_ref),
@@ -210,6 +218,8 @@
     lax.fori_loop(1, n_wide, greet_wide, 0)
     lax.fori_loop(1, n_narrow, greet_narrow, 0)
 
+    loads[0].wait()
+    loads[1].wait()
     brick_col[...] = jnp.zeros_like(brick_col)
 
     def spread(b, carry):
@@ -229,29 +239,24 @@
     slot_t = jnp.transpose(slot.astype(jnp.float32)).astype(jnp.int32)
     by = (bricks >> 5) & 31
     place = ((by >> 4) * 64 + (bricks & 3) * 16 + (by & 15) + 1).astype(jnp.bfloat16)
-    wide_row = lax.broadcasted_iota(jnp.int32, (n_wide * 8, 128), 0)
-    wanted = jnp.where((wide_row & 7) < 2, (wide_row >> 3) * 2 + (wide_row & 7), -2)
-    pick8 = jnp.where(
-        jnp.broadcast_to(slot_t[0:1], (n_wide * 8, 128)) == wanted, 1.0, 0.0
-    ).astype(jnp.bfloat16)
-    place_send[...] = (
-        jnp.dot(pick8, place, preferred_element_type=jnp.float32) - 1.0
-    )
     slot_row = lax.broadcasted_iota(jnp.int32, (2 * n_wide, 128), 0)
     slot_row = jnp.where(slot_row < n_wide, 2 * slot_row, 2 * (slot_row - n_wide) + 1)
     pick = jnp.where(
         jnp.broadcast_to(slot_t[0:1], (2 * n_wide, 128)) == slot_row, 1.0, 0.0
     ).astype(jnp.bfloat16)[:, :32]
+    first = lax.broadcasted_iota(jnp.int32, (32, 128), 1) < 64
+    places = jnp.dot(pick, place[:32], preferred_element_type=jnp.float32) - 1.0
+    place_send[:, 0, :] = jnp.where(first, places[:n_wide], places[n_wide:])
     pick = jnp.concatenate([pick, pick], 1)
 
-    loads[0].wait()
-    loads[1].wait()
+    loads[2].wait()
+    loads[3].wait()
     for g in range(waves_ref.shape[0]):
         at = slice(g * GRP, g * GRP + GRP)
         waves_ref[g, 0:3, :] = freq_ref[:, at]
         waves_ref[g, 3:6, :] = phase_ref[:, at]
         waves_ref[g, 6:8, :] = jnp.zeros((2, GRP), jnp.float32)
-    loads[2].wait()
+    loads[4].wait()
     piece_ref[...] = jnp.zeros_like(piece_ref)
 
     def prepare(b, carry):
@@ -262,15 +267,13 @@
 
     lax.fori_loop(0, n_blocks, prepare, 0, unroll=4)
 
-    first = lax.broadcasted_iota(jnp.int32, (32, 128), 1) < 64
-
     def place_copy(d):
         peer = lax.rem(wide + d, n_wide)
         return pltpu.make_async_remote_copy(
-            src_ref=place_send.at[pl.ds(pl.multiple_of(peer * 8, 8), 8)],
-            dst_ref=place_recv.at[pl.ds(pl.multiple_of(wide * 8, 8), 8)],
-            send_sem=place_ssem.at[d],
-            recv_sem=place_rsem.at[d],
+            src_ref=place_send.at[peer],
+            dst_ref=place_recv.at[wide],
+            send_sem=place_ssem,
+            recv_sem=place_rsem,
             device_id=(peer, narrow),
             device_id_type=MESH,
         )
@@ -280,8 +283,8 @@
         return pltpu.make_async_remote_copy(
             src_ref=send_ref.at[h, pl.ds(pl.multiple_of(peer * 8, 8), 8)],
             dst_ref=recv_ref.at[h, pl.ds(pl.multiple_of(wide * 8, 8), 8)],
-            send_sem=piece_ssem.at[h, d],
-            recv_sem=piece_rsem.at[h, d],
+            send_sem=piece_ssem.at[h],
+            recv_sem=piece_rsem.at[h],
             device_id=(peer, narrow),
             device_id_type=MESH,
         )
@@ -318,9 +321,9 @@
                 return carry
 
             lax.fori_loop(1, n_wide, start_place, 0)
-            place_recv[own8] = place_send[own8]
-
-    loads[3].wait()
+            place_recv[wide] = place_send[wide]
+
+    loads[5].wait()
     at = lax.broadcasted_iota(jnp.int32, (256, 256), 0)
     to = (
         ((at >> 4) & 1) * 128 + (at >> 7) * 64 + ((at >> 5) & 3) * 16 + (at & 15)
@@ -353,14 +356,12 @@
             core_part[h, r * 128 : r * 128 + 128, :] = own
             core_pow[h, r * 128 : r * 128 + 128, :] = power43(own)
 
-    def wait_place(d, carry):
-        place_copy(d).wait()
-        return carry
-
-    lax.fori_loop(1, n_wide, wait_place, 0)
+    wait_all(place_recv.at[pl.ds(0, n_wide - 1)], place_rsem)
+    wait_all(place_send.at[pl.ds(0, n_wide - 1)], place_ssem)
+    places = place_recv[:, 0, :]
     brick_lane = lax.broadcasted_iota(jnp.int32, (n_wide, 128), 1).astype(jnp.float32)
     spots = [
-        jnp.where(place_recv[pl.ds(k, n_wide, stride=8), :] == brick_lane, 1.0, 0.0)
+        jnp.where(places[:, k * 64 : k * 64 + 1] == brick_lane, 1.0, 0.0)
         for k in range(2)
     ]
     gather = jnp.transpose(jnp.concatenate([*spots, *spots], 0)).astype(jnp.bfloat16)
@@ -387,12 +388,9 @@
     low16 = group < 4
     low64 = lax.broadcasted_iota(jnp.int32, (64, 128), 1) < 64
     for h in range(2):
-
-        def wait_piece(d, carry, h=h):
-            piece_copy(h, d).wait()
-            return carry
-
-        lax.fori_loop(1, n_wide, wait_piece, 0)
+        others = pl.ds(0, (n_wide - 1) * 8)
+        wait_all(recv_ref.at[h, others], piece_rsem.at[h])
+        wait_all(send_ref.at[h, others], piece_ssem.at[h])
         for r in range(4):
             even = recv_ref[h, pl.ds(2 * r, n_wide, stride=8), :]
             odd = recv_ref[h, pl.ds(2 * r + 1, n_wide, stride=8), :]
@@ -433,7 +431,7 @@
                     low16, pltpu.roll(high, 64, 1), rest
                 ).astype(jnp.bfloat16)
         if h == 0:
-            loads[4].wait()
+            loads[6].wait()
         for i, hop in enumerate(hops):
             peer = peer_at(hop)
             target = half_recv.at[h, narrow] if hop == (0, 0) else half_send.at[h, peer]
@@ -454,7 +452,7 @@
             if hop != (0, 0):
                 half_copy(h, i).start()
 
-    loads[5].wait()
+    loads[7].wait()
     low256 = (lax.broadcasted_iota(jnp.int32, (128, 256), 1) & 127) < 64
     waits = {0: (6,), 1: (3, 5), 3: (2, 4), 2: (0, 1)}
     for h in range(2):
@@ -492,16 +490,17 @@
     n_blocks = density_blocks.shape[0]
     ytab, xtab = y_tables(n_narrow), x_tables(n_narrow // 2)
     vmem = pl.BlockSpec(memory_space=pltpu.VMEM)
-    smem = pl.BlockSpec(memory_space=pltpu.SMEM)
-    hbm = pl.BlockSpec(memory_space=pl.ANY)
+    hbm = pl.BlockSpec(memory_space=pltpu.HBM)
     f32, bf16 = jnp.float32, jnp.bfloat16
     rows = NY // n_narrow
     return pl.pallas_call(
         functools.partial(whole_kernel, n_wide, n_narrow, n_blocks),
         out_shape=jax.ShapeDtypeStruct((1, 2, rows, NX // 2), f32),
-        in_specs=[smem, smem, hbm, hbm, hbm, hbm, hbm, hbm],
+        in_specs=[hbm] * 8,
         out_specs=vmem,
         scratch_shapes=[
+            pltpu.SMEM((2, n_blocks), jnp.int32),
+            pltpu.SMEM((n_blocks,), jnp.int32),
             pltpu.VMEM(orbital_freq.shape, f32),
             pltpu.VMEM(orbital_phase.shape, f32),
             pltpu.VMEM(density_blocks.shape, f32),
@@ -513,8 +512,8 @@
             pltpu.VMEM((n_blocks, 2 * GRP, 2 * GRP), bf16),
             pltpu.VMEM((128, 128), jnp.int32),
             pltpu.VMEM((2, 32 * 8, 128), f32),
-            pltpu.VMEM((n_wide * 8, 128), f32),
-            pltpu.VMEM((n_wide * 8, 128), f32),
+            pltpu.VMEM((n_wide, 1, 128), f32),
+            pltpu.VMEM((n_wide, 1, 128), f32),
             pltpu.VMEM((2, n_wide * 8, 128), f32),
             pltpu.VMEM((2, n_wide * 8, 128), f32),
             pltpu.VMEM((2, NY // 2, 128), f32),
@@ -523,26 +522,31 @@
             pltpu.VMEM((2, n_narrow, 128, 128), f32),
             pltpu.VMEM((2, n_narrow, 128, 128), f32),
             pltpu.VMEM((256, NX // 2), f32),
-            pltpu.SemaphoreType.DMA((6,)),
-            pltpu.SemaphoreType.DMA((n_wide,)),
-            pltpu.SemaphoreType.DMA((n_wide,)),
-            pltpu.SemaphoreType.DMA((2, n_wide)),
-            pltpu.SemaphoreType.DMA((2, n_wide)),
+            pltpu.SemaphoreType.DMA((8,)),
+            pltpu.SemaphoreType.DMA,
+            pltpu.SemaphoreType.DMA,
+            pltpu.SemaphoreType.DMA((2,)),
+            pltpu.SemaphoreType.DMA((2,)),
             pltpu.SemaphoreType.DMA((2, n_narrow)),
             pltpu.SemaphoreType.DMA((2, n_narrow)),
         ],
         compiler_params=pltpu.CompilerParams(
-            collective_id=0, has_side_effects=True, vmem_limit_bytes=62 * 2**20
+            collective_id=0, has_side_effects=True, vmem_limit_bytes=48 * 2**20
         ),
     )(
-        block_groups.T,
-        block_brick,
-        orbital_freq,
-        orbital_phase,
-        density_blocks,
-        core_density.reshape(core_density.shape[1:]),
-        jnp.asarray(ytab),
-        jnp.asarray(xtab),
+        *(
+            pltpu.with_memory_space_constraint(array, pltpu.HBM)
+            for array in (
+                block_groups.T,
+                block_brick,
+                orbital_freq,
+                orbital_phase,
+                density_blocks,
+                core_density.reshape(core_density.shape[1:]),
+                jnp.asarray(ytab),
+                jnp.asarray(xtab),
+            )
+        ),
     )
 
 

time: 43.1 us -> 37.5 us (0.87)
  Pallas kernels: 41.1 us -> 36.6 us
  local copies, waits for them, and re-layouts: 1.87 us -> 0.8 us
    pallas_call x1, Pallas kernels: 41.1 us -> 36.6 us  [local(): pl.pallas_call(functools.partial(whole_kernel, n_wide, n_narrow, n_blocks...]
    unnamed x1, local copies, waits for them, and re-layouts: 1.87 us -> 0.8 us
where the time goes in v3:
time: 37.5 us
  Pallas kernels  36.6 us (98%)
  local copies, waits for them, and re-layouts  0.8 us (2%)
    pallas_call x1, Pallas kernels, local(): pl.pallas_call(functools.partial(whole_kernel, n_wide, n_narrow, n_blocks...  36.6 us
    unnamed x1, local copies, waits for them, and re-layouts  0.8 us

profile of v3, /device:TPU:1, one launch (start us, length us, event | category | flops | bytes accessed | tf_op | source)
XLA Modules:
  0.0 37.5 jit_solution(2008202121943884389)
XLA Ops:
  0.0 36.6 %shard_map.82 = f32[1,2,128,512]{3,2,1,0:T(8,128)S(1)} custom-call(s32[2,24]{1,0:T(2,128)} %bitcast.3, s32[24]{0:T(128)} %brick_hbm.1, f32[3,8192]{1,0:T(4,128)} %freq_hbm.1, f32[3,8192]{1,0:T(4,128)} %phase_hbm.1, f32[24,128,128]{2,1,0:T(8,128)} %blocks_hbm.1, f32[1024,128]{1,0:T(8,128)} %bitcast.2, bf16[2,8,2,128,512]{4,3,2,1,0:T(8,128)(2,1)} %constant.4.clone.ytab_hbm, ...), custom_call_target="tpu_custom_call" | custom-call | tf_op jit(solution)/shard_map/pallas_call | solution.py:496
  36.7 0.8 %copy.10 = f32[1,2,128,512]{3,2,1,0:T(8,128)} copy(f32[1,2,128,512]{3,2,1,0:T(8,128)S(1)} %shard_map.82) | data formatting | bytes 1048576

commit v4 on v3

--- a/solution.py
+++ b/solution.py
@@ -87,7 +87,7 @@
     pltpu.make_async_copy(ref, ref, sem).wait()
 
 
-def block_tables(b, groups_ref, brick_ref, waves_ref, blocks_ref, factor_ref, weight_ref):
+def block_factors(b, groups_ref, brick_ref, waves_ref, factor_ref):
     brick = brick_ref[b]
     x0 = ((brick & 31) * BX).astype(jnp.float32)
     y0 = (((brick >> 5) & 31) * BY).astype(jnp.float32)
@@ -99,6 +99,9 @@
         along_z = cosine(z0 * wave[2:3] + wave[5:6])
         factor_ref[b, 2 * side] = cosine(xs * wave[0:1] + wave[3:4]) * along_z
         factor_ref[b, 2 * side + 1] = cosine(ys * wave[1:2] + wave[4:5])
+
+
+def block_halves(b, blocks_ref, weight_ref):
     high, low = split(blocks_ref[b])
     weight_ref[b] = jnp.concatenate(
         [
@@ -196,7 +199,7 @@
             )
         )
     ]
-    for load in loads:
+    for load in loads[:5]:
         load.start()
 
     barrier = pltpu.get_barrier_semaphore()
@@ -256,16 +259,22 @@
         waves_ref[g, 0:3, :] = freq_ref[:, at]
         waves_ref[g, 3:6, :] = phase_ref[:, at]
         waves_ref[g, 6:8, :] = jnp.zeros((2, GRP), jnp.float32)
+    piece_ref[...] = jnp.zeros_like(piece_ref)
+
+    def prepare(b, carry):
+        block_factors(b, groups_ref, brick_ref, waves_ref, factor_ref)
+        return carry
+
+    lax.fori_loop(0, n_blocks, prepare, 0, unroll=4)
     loads[4].wait()
-    piece_ref[...] = jnp.zeros_like(piece_ref)
-
-    def prepare(b, carry):
-        block_tables(
-            b, groups_ref, brick_ref, waves_ref, blocks_ref, factor_ref, weight_ref
-        )
+    for load in loads[5:]:
+        load.start()
+
+    def halve(b, carry):
+        block_halves(b, blocks_ref, weight_ref)
         return carry
 
-    lax.fori_loop(0, n_blocks, prepare, 0, unroll=4)
+    lax.fori_loop(0, n_blocks, halve, 0, unroll=4)
 
     def place_copy(d):
         peer = lax.rem(wide + d, n_wide)
@@ -290,9 +299,9 @@
         )
 
     own8 = pl.ds(pl.multiple_of(wide * 8, 8), 8)
-    for h in range(2):
-
-        def work(b, carry, h=h):
+
+    def compute_half(h):
+        def work(b, carry):
             piece_ref[h, pl.ds(pl.multiple_of(b * 8, 8), 8), :] = half_piece(
                 b, h, factor_ref, weight_ref
             )
@@ -305,23 +314,25 @@
             send_ref[h, pl.ds(r, n_wide, stride=8), :] = jnp.where(
                 first, slots[:n_wide], slots[n_wide:]
             )
-        if h == 0:
-            pl.semaphore_wait(barrier, n_wide + n_narrow - 2)
-
-        def start_piece(d, carry, h=h):
+
+    def send_half(h):
+        def start_piece(d, carry):
             piece_copy(h, d).start()
             return carry
 
         lax.fori_loop(1, n_wide, start_piece, 0)
         recv_ref[h, own8] = send_ref[h, own8]
-        if h == 0:
-
-            def start_place(d, carry):
-                place_copy(d).start()
-                return carry
-
-            lax.fori_loop(1, n_wide, start_place, 0)
-            place_recv[wide] = place_send[wide]
+
+    compute_half(0)
+    pl.semaphore_wait(barrier, n_wide + n_narrow - 2)
+    send_half(0)
+
+    def start_place(d, carry):
+        place_copy(d).start()
+        return carry
+
+    lax.fori_loop(1, n_wide, start_place, 0)
+    place_recv[wide] = place_send[wide]
 
     loads[5].wait()
     at = lax.broadcasted_iota(jnp.int32, (256, 256), 0)
@@ -356,6 +367,8 @@
             core_part[h, r * 128 : r * 128 + 128, :] = own
             core_pow[h, r * 128 : r * 128 + 128, :] = power43(own)
 
+    compute_half(1)
+    send_half(1)
     wait_all(place_recv.at[pl.ds(0, n_wide - 1)], place_rsem)
     wait_all(place_send.at[pl.ds(0, n_wide - 1)], place_ssem)
     places = place_recv[:, 0, :]
@@ -367,7 +380,7 @@
     gather = jnp.transpose(jnp.concatenate([*spots, *spots], 0)).astype(jnp.bfloat16)
 
     chips = n_narrow // 2
-    hops = [(2, 0), (2, 1), (1, 0), (3, 0), (1, 1), (3, 1), (0, 1), (0, 0)]
+    hops = [(1, 0), (3, 0), (1, 1), (3, 1), (2, 0), (2, 1), (0, 1), (0, 0)]
 
     def peer_at(hop):
         chip = lax.rem(narrow // 2 + hop[0], chips)
@@ -454,7 +467,7 @@
 
     loads[7].wait()
     low256 = (lax.broadcasted_iota(jnp.int32, (128, 256), 1) & 127) < 64
-    waits = {0: (6,), 1: (3, 5), 3: (2, 4), 2: (0, 1)}
+    waits = {0: (6,), 1: (1, 3), 3: (0, 2), 2: (4, 5)}
     for h in range(2):
         for on, copies in waits.items():
             for i in copies:

time: 37.5 us -> 37 us (0.987)
  Pallas kernels: 36.6 us -> 36.1 us
    pallas_call x1, Pallas kernels: 36.6 us -> 36.1 us  [local(): pl.pallas_call(functools.partial(whole_kernel, n_wide, n_narrow, n_blocks...]
where the time goes in v4:
time: 37 us; the launch traced here: 36.9 us
  Pallas kernels  36.1 us (98%)
  local copies, waits for them, and re-layouts  0.8 us (2%)
    pallas_call x1, Pallas kernels, local(): pl.pallas_call(functools.partial(whole_kernel, n_wide, n_narrow, n_blocks...  36.1 us
    unnamed x1, local copies, waits for them, and re-layouts  0.8 us

profile of v4, /device:TPU:1, one launch (start us, length us, event | category | flops | bytes accessed | tf_op | source)
XLA Modules:
  0.0 36.9 jit_solution(4750431453184110211)
XLA Ops:
  0.0 36.1 %shard_map.82 = f32[1,2,128,512]{3,2,1,0:T(8,128)S(1)} custom-call(s32[2,24]{1,0:T(2,128)} %bitcast.3, s32[24]{0:T(128)} %brick_hbm.1, f32[3,8192]{1,0:T(4,128)} %freq_hbm.1, f32[3,8192]{1,0:T(4,128)} %phase_hbm.1, f32[24,128,128]{2,1,0:T(8,128)} %blocks_hbm.1, f32[1024,128]{1,0:T(8,128)} %bitcast.2, bf16[2,8,2,128,512]{4,3,2,1,0:T(8,128)(2,1)} %constant.4.clone.ytab_hbm, ...), custom_call_target="tpu_custom_call" | custom-call | tf_op jit(solution)/shard_map/pallas_call | solution.py:509
  36.1 0.8 %copy.10 = f32[1,2,128,512]{3,2,1,0:T(8,128)} copy(f32[1,2,128,512]{3,2,1,0:T(8,128)S(1)} %shard_map.82) | data formatting | bytes 1048576

commit v5 on v4

--- a/solution.py
+++ b/solution.py
@@ -308,11 +308,13 @@
             return carry
 
         lax.fori_loop(0, n_blocks, work, 0, unroll=8)
+        rows = [piece_ref[h, pl.ds(r, 32, stride=8), :] for r in range(8)]
+        both = jnp.concatenate(split(jnp.concatenate(rows, 1)), 0)
+        slots = jnp.dot(pick, both, preferred_element_type=jnp.float32)
         for r in range(8):
-            both = jnp.concatenate(split(piece_ref[h, pl.ds(r, 32, stride=8), :]), 0)
-            slots = jnp.dot(pick, both, preferred_element_type=jnp.float32)
+            at = slice(r * 128, r * 128 + 128)
             send_ref[h, pl.ds(r, n_wide, stride=8), :] = jnp.where(
-                first, slots[:n_wide], slots[n_wide:]
+                first, slots[:n_wide, at], slots[n_wide:, at]
             )
 
     def send_half(h):
@@ -404,6 +406,7 @@
         others = pl.ds(0, (n_wide - 1) * 8)
         wait_all(recv_ref.at[h, others], piece_rsem.at[h])
         wait_all(send_ref.at[h, others], piece_ssem.at[h])
+        halves = []
         for r in range(4):
             even = recv_ref[h, pl.ds(2 * r, n_wide, stride=8), :]
             odd = recv_ref[h, pl.ds(2 * r + 1, n_wide, stride=8), :]
@@ -414,11 +417,12 @@
                 ],
                 0,
             )
-            sums = jnp.dot(
-                gather,
-                jnp.concatenate(split(got), 0),
-                preferred_element_type=jnp.float32,
-            )
+            halves.append(jnp.concatenate(split(got), 0))
+        all_sums = jnp.dot(
+            gather, jnp.concatenate(halves, 1), preferred_element_type=jnp.float32
+        )
+        for r in range(4):
+            sums = all_sums[:, r * 128 : r * 128 + 128]
             tiles = [sums[j * 16 : j * 16 + 16] for j in range(8)]
             for bit in (1, 2, 4):
                 for j in range(8):

time: 37 us -> 37 us (level)
  no operation moved by 1% of the time
where the time goes in v5:
time: 37 us
  Pallas kernels  36.1 us (98%)
  local copies, waits for them, and re-layouts  0.8 us (2%)
    pallas_call x1, Pallas kernels, local(): pl.pallas_call(functools.partial(whole_kernel, n_wide, n_narrow, n_blocks...  36.1 us
    unnamed x1, local copies, waits for them, and re-layouts  0.8 us

profile of v5, /device:TPU:1, one launch (start us, length us, event | category | flops | bytes accessed | tf_op | source)
XLA Modules:
  0.0 37.0 jit_solution(14884823195974767682)
XLA Ops:
  0.0 36.1 %shard_map.82 = f32[1,2,128,512]{3,2,1,0:T(8,128)S(1)} custom-call(s32[2,24]{1,0:T(2,128)} %bitcast.3, s32[24]{0:T(128)} %brick_hbm.1, f32[3,8192]{1,0:T(4,128)} %freq_hbm.1, f32[3,8192]{1,0:T(4,128)} %phase_hbm.1, f32[24,128,128]{2,1,0:T(8,128)} %blocks_hbm.1, f32[1024,128]{1,0:T(8,128)} %bitcast.2, bf16[2,8,2,128,512]{4,3,2,1,0:T(8,128)(2,1)} %constant.4.clone.ytab_hbm, ...), custom_call_target="tpu_custom_call" | custom-call | tf_op jit(solution)/shard_map/pallas_call | solution.py:513
  36.2 0.8 %copy.10 = f32[1,2,128,512]{3,2,1,0:T(8,128)} copy(f32[1,2,128,512]{3,2,1,0:T(8,128)S(1)} %shard_map.82) | data formatting | bytes 1048576

commit v6 on v5

--- a/solution.py
+++ b/solution.py
@@ -372,7 +372,6 @@
     compute_half(1)
     send_half(1)
     wait_all(place_recv.at[pl.ds(0, n_wide - 1)], place_rsem)
-    wait_all(place_send.at[pl.ds(0, n_wide - 1)], place_ssem)
     places = place_recv[:, 0, :]
     brick_lane = lax.broadcasted_iota(jnp.int32, (n_wide, 128), 1).astype(jnp.float32)
     spots = [
@@ -405,7 +404,6 @@
     for h in range(2):
         others = pl.ds(0, (n_wide - 1) * 8)
         wait_all(recv_ref.at[h, others], piece_rsem.at[h])
-        wait_all(send_ref.at[h, others], piece_ssem.at[h])
         halves = []
         for r in range(4):
             even = recv_ref[h, pl.ds(2 * r, n_wide, stride=8), :]
@@ -497,7 +495,9 @@
                 for c in range(2):
                     out_ref[0, c] = total[c * 128 : c * 128 + 128]
 
+    wait_all(place_send.at[pl.ds(0, n_wide - 1)], place_ssem)
     for h in range(2):
+        wait_all(send_ref.at[h, pl.ds(0, (n_wide - 1) * 8)], piece_ssem.at[h])
         for i in range(len(hops) - 1):
             half_copy(h, i).wait_send()
 

time: 37 us -> 37 us (level)
  no operation moved by 1% of the time
where the time goes in v6:
time: 37 us; the launch traced here: 36.9 us
  Pallas kernels  36.1 us (98%)
  local copies, waits for them, and re-layouts  0.8 us (2%)
    pallas_call x1, Pallas kernels, local(): pl.pallas_call(functools.partial(whole_kernel, n_wide, n_narrow, n_blocks...  36.1 us
    unnamed x1, local copies, waits for them, and re-layouts  0.8 us

profile of v6, /device:TPU:1, one launch (start us, length us, event | category | flops | bytes accessed | tf_op | source)
XLA Modules:
  0.0 36.9 jit_solution(4738620781411084579)
XLA Ops:
  0.0 36.1 %shard_map.82 = f32[1,2,128,512]{3,2,1,0:T(8,128)S(1)} custom-call(s32[2,24]{1,0:T(2,128)} %bitcast.3, s32[24]{0:T(128)} %brick_hbm.1, f32[3,8192]{1,0:T(4,128)} %freq_hbm.1, f32[3,8192]{1,0:T(4,128)} %phase_hbm.1, f32[24,128,128]{2,1,0:T(8,128)} %blocks_hbm.1, f32[1024,128]{1,0:T(8,128)} %bitcast.2, bf16[2,8,2,128,512]{4,3,2,1,0:T(8,128)(2,1)} %constant.4.clone.ytab_hbm, ...), custom_call_target="tpu_custom_call" | custom-call | tf_op jit(solution)/shard_map/pallas_call | solution.py:513
  36.1 0.8 %copy.10 = f32[1,2,128,512]{3,2,1,0:T(8,128)} copy(f32[1,2,128,512]{3,2,1,0:T(8,128)S(1)} %shard_map.82) | data formatting | bytes 1048576
